TPU v7x, 128 devices: a whole 4x4x4 slice. The times are simulated.
128 devices in a mesh: dp: 16 (over z, x_hi, core), tensor: 8 (over x_lo, y).
Axes of the slice: x: 4 (x_hi: 2, x_lo: 2; x = x_hi * 2 + x_lo), y: 4, z: 4, core: 2. Of those that a mesh axis runs over, the one named last changes fastest.
Arguments:
- resid_in: bfloat16 [32768, 768], P(('dp', 'tensor')), may hold values from -6 to 6
- cotangent: bfloat16 [32768, 768], P(('dp', 'tensor')), may hold values from -6 to 6
- segments: int32 [32768], P('dp'), may hold values from 0 to 3, as said below
- in_gain: float32 [768], replicated, may hold values from 0.5 to 1.5
- w_gate: bfloat16 [768, 1536], P('dp', 'tensor'), may hold values from -0.21875 to 0.21875
- w_value: bfloat16 [768, 1536], P('dp', 'tensor'), may hold values from -0.21875 to 0.21875
- w_step: bfloat16 [768, 24], P('dp', 'tensor'), may hold values from -0.21875 to 0.21875
- w_shared: bfloat16 [768, 256], replicated, may hold values from -0.21875 to 0.21875
- conv_inner: float32 [4, 1536], P(None, 'tensor'), may hold values from -0.5 to 0.5
- bias_inner: float32 [1536], P('tensor'), may hold values from -0.5 to 0.5
- conv_shared: float32 [4, 256], replicated, may hold values from -0.5 to 0.5
- bias_shared: float32 [256], replicated, may hold values from -0.5 to 0.5
- step_bias: float32 [24], P('tensor'), may hold values from -3 to -2
- decay_log: float32 [24], P('tensor'), may hold values from -9 to -0.8
- skip_gain: float32 [24], P('tensor'), may hold values from 0.5 to 1.5
- out_gain: float32 [1536], P('tensor'), may hold values from 0.5 to 1.5
- w_out: bfloat16 [768, 1536], P('dp', 'tensor'), may hold values from -0.15625 to 0.15625
Outputs:
- result: bfloat16 [32768, 768], P(('dp', 'tensor'))
- grad_resid: float32 [32768, 768], P(('dp', 'tensor'))
- grad_in_gain: float32 [768], replicated
- grad_w_gate: float32 [768, 1536], P('dp', 'tensor')
- grad_w_value: float32 [768, 1536], P('dp', 'tensor')
- grad_w_step: float32 [768, 24], P('dp', 'tensor')
- grad_w_shared: float32 [768, 256], replicated
- grad_conv_inner: float32 [4, 1536], P(None, 'tensor')
- grad_bias_inner: float32 [1536], P('tensor')
- grad_conv_shared: float32 [4, 256], replicated
- grad_bias_shared: float32 [256], replicated
- grad_step_bias: float32 [24], P('tensor')
- grad_decay_log: float32 [24], P('tensor')
- grad_skip_gain: float32 [24], P('tensor')
- grad_out_gain: float32 [1536], P('tensor')
- grad_w_out: float32 [768, 1536], P('dp', 'tensor')
Inputs may be any that keep to these rules, and one draw needn't show every extreme that they name: `segments`: each sequence holds four documents numbered 0 to 3 in order, each of 256 tokens or more.
All inputs are finite; a program needn't handle non-finite values.
Results may differ from a plain program's by a relative error of at most 0.022.
Values may be sent and summed in bfloat16 or wider, within the bound.
A program may use at most 128 MiB of HBM per device.

v0:
```python
import jax
import jax.numpy as jnp
from jax import lax
from jax.sharding import PartitionSpec as P

HEADDIM = 64
STATE = 128
GROUP = 256
INNER = 1536


HIGHEST = lax.Precision.HIGHEST
EPSILON = 1e-05


def side_by_side(arrays, axis, dim, along):
    both = jnp.concatenate(arrays, axis=along)
    result, at, finished = (lax.all_gather(both, axis, axis=dim, tiled=True), 0, [])
    for a in arrays:
        finished.append(lax.slice_in_dim(result, at, at + a.shape[along], axis=along))
        at += a.shape[along]
    return tuple(finished)


def copy_for_each(value, axis):
    length = lax.axis_size(axis)
    return lax.all_to_all(
        jnp.broadcast_to(value[None], (length, *value.shape)), axis, 0, 0, tiled=True
    )


def of_everyone(value, axis):
    return copy_for_each(value, axis).sum(axis=0)


def split_up(value, dim, length):
    dims = value.shape
    pieces = value.reshape(*dims[:dim], length, dims[dim] // length, *dims[dim + 1 :])
    return jnp.moveaxis(pieces, dim, 0)


def sent_and_summed(value, axis, dim):
    pieces = split_up(value, dim, lax.axis_size(axis))
    arrived = lax.all_to_all(pieces, axis, split_axis=0, concat_axis=0, tiled=True)
    return arrived.sum(axis=0)


def side_by_side_2(arrays, axis, dim, along):
    both = jnp.concatenate(arrays, axis=along)
    result, at, finished = (lax.psum_scatter(both, axis, scatter_dimension=dim, tiled=True), 0, [])
    for a in arrays:
        finished.append(lax.slice_in_dim(result, at, at + a.shape[along], axis=along))
        at += a.shape[along]
    return tuple(finished)


def together(arrays, axis):
    ends = [0]
    for a in arrays:
        ends.append(ends[-1] + a.size)
    total = of_everyone(jnp.concatenate([a.ravel() for a in arrays]), axis)
    return tuple((total[b:e].reshape(a.shape) for a, b, e in zip(arrays, ends, ends[1:])))


def causal_conv(before, weight, offset, segment):
    taps, channels = weight.shape
    summed = offset[None, :] + weight[taps - 1][None, :] * before
    for back in range(1, taps):
        shifted = jnp.concatenate([jnp.zeros((back, channels), before.dtype), before[:-back]], 0)
        earlier = jnp.concatenate([jnp.full((back,), -1, jnp.int32), segment[:-back]], 0)
        usable = (earlier == segment)[:, None]
        summed = summed + weight[taps - 1 - back][None, :] * jnp.where(usable, shifted, 0.0)
    return jax.nn.silu(summed)


def block_scan(values, bees, cees, step_values, step_offset, decay, skip, segment):
    length, heads, width = values.shape
    blocks = length // GROUP
    steps = jax.nn.softplus(step_values + step_offset[None, :])
    rates = steps * (-jnp.exp(decay))[None, :]

    def split(array):
        return array.reshape((blocks, GROUP) + array.shape[1:])

    causal = jnp.arange(GROUP)[:, None] >= jnp.arange(GROUP)[None, :]

    def advance(carry, block):
        state, last_id = carry
        vals, bmat, cmat, step_blk, rate_blk, ident = block
        logs = jnp.cumsum(rate_blk.T, axis=1)
        allowed = (causal & (ident[:, None] == ident[None, :]))[None]
        gaps = logs[:, :, None] - logs[:, None, :]
        decays = jnp.where(allowed, jnp.exp(jnp.where(allowed, gaps, 0.0)), 0.0)
        scores = jnp.dot(cmat, bmat.T, precision=HIGHEST)
        mixing = scores[None] * decays * step_blk.T[:, None, :]
        inside = jnp.einsum("hts,shp->thp", mixing, vals, precision=HIGHEST)
        joined = (ident == last_id)[None, :]
        carried = jnp.where(joined, jnp.exp(logs), 0.0)
        from_state = (
            jnp.einsum("tn,hnp->thp", cmat, state, precision=HIGHEST) * carried.T[:, :, None]
        )
        ending = (ident == ident[-1])[None, :]
        weights = jnp.where(ending, jnp.exp(logs[:, -1:] - logs), 0.0) * step_blk.T
        fresh = jnp.einsum("sn,hs,shp->hnp", bmat, weights, vals, precision=HIGHEST)
        kept = jnp.where(ident[-1] == last_id, jnp.exp(logs[:, -1]), 0.0)
        state = fresh + state * kept[:, None, None]
        return ((state, ident[-1]), inside + from_state)

    start = (jnp.zeros((heads, bees.shape[1], width), values.dtype), jnp.int32(-1))
    ignored, outputs = lax.scan(
        jax.checkpoint(advance),
        start,
        (split(values), split(bees), split(cees), split(steps), split(rates), split(segment)),
    )
    return outputs.reshape(length, heads, width) + skip[None, :, None] * values


def contract_last(left, right):
    return lax.dot_general(
        left, right, (((1,), (1,)), ((), ())), preferred_element_type=jnp.float32
    )


def contract_first(left, right):
    return lax.dot_general(
        left, right, (((0,), (0,)), ((), ())), preferred_element_type=jnp.float32
    )


def shards(
    resid_in,
    cotangent,
    segments,
    in_gain,
    w_gate,
    w_value,
    w_step,
    w_shared,
    conv_inner,
    bias_inner,
    conv_shared,
    bias_shared,
    step_bias,
    decay_log,
    skip_gain,
    out_gain,
    w_out,
):
    heads_local = w_step.shape[1]
    own_in = resid_in.astype(jnp.float32)
    mean_sq = jnp.mean(own_in * own_in, axis=1, keepdims=True)
    inverse_in = lax.rsqrt(mean_sq + EPSILON)
    scaled = own_in * inverse_in
    normed_own = (scaled * in_gain[None, :]).astype(jnp.bfloat16)
    normed = lax.all_gather(normed_own, "tensor", axis=0, tiled=True)
    length = normed.shape[0]
    full_gate, full_value, full_step, full_out = side_by_side(
        (w_gate, w_value, w_step, w_out), "dp", 0, 1
    )
    gate_pre = jnp.dot(normed, full_gate, preferred_element_type=jnp.float32)
    value_pre = jnp.dot(normed, full_value, preferred_element_type=jnp.float32)
    step_raw = jnp.dot(normed, full_step, preferred_element_type=jnp.float32)
    shared_pre = jnp.dot(normed, w_shared, preferred_element_type=jnp.float32)

    def inner_conv(before, weight, offset):
        return causal_conv(before, weight, offset, segments)

    inner_act, inner_pull = jax.vjp(inner_conv, value_pre, conv_inner, bias_inner)
    shared_act, shared_pull = jax.vjp(inner_conv, shared_pre, conv_shared, bias_shared)
    inner_low = inner_act.astype(jnp.bfloat16)
    shared_low = shared_act.astype(jnp.bfloat16)

    def ssd_local(values, bmat, cmat, step_values, step_offset, decay, skip):
        return block_scan(values, bmat, cmat, step_values, step_offset, decay, skip, segments)

    inner_wide = inner_low.astype(jnp.float32).reshape(length, heads_local, HEADDIM)
    shared_wide = shared_low.astype(jnp.float32)
    mixed, ssd_pull = jax.vjp(
        ssd_local,
        inner_wide,
        shared_wide[:, :STATE],
        shared_wide[:, STATE:],
        step_raw,
        step_bias,
        decay_log,
        skip_gain,
    )
    mixed = mixed.reshape(length, heads_local * HEADDIM)
    silu_gate = jax.nn.silu(gate_pre)
    gated = mixed * silu_gate
    square_total = of_everyone(jnp.sum(gated * gated, axis=1, keepdims=True), "tensor")
    inverse = lax.rsqrt(square_total / INNER + EPSILON)
    normed_out = (gated * inverse * out_gain[None, :]).astype(jnp.bfloat16)
    gate_all, value_all, step_all, out_all = (
        *side_by_side((full_gate, full_value), "tensor", 1, 0),
        lax.all_gather(full_step, "tensor", axis=1, tiled=True),
        lax.all_gather(full_out, "tensor", axis=1, tiled=True),
    )
    out_rows = lax.all_to_all(normed_out, "tensor", split_axis=0, concat_axis=1, tiled=True)
    branch = contract_last(out_rows, out_all)
    result = (own_in + branch).astype(jnp.bfloat16)
    cot_full = lax.all_gather(cotangent, "tensor", axis=0, tiled=True)
    out_weight_part = contract_first(cot_full, normed_out)
    d_out = jnp.dot(cot_full, full_out, preferred_element_type=jnp.float32)
    out_gain_part = jnp.sum(d_out * gated * inverse, axis=0)
    d_scaled = d_out * out_gain[None, :]
    dot_total = of_everyone(jnp.sum(d_scaled * gated, axis=1, keepdims=True), "tensor")
    d_gated = inverse * d_scaled - gated * inverse * inverse * inverse * dot_total / INNER
    d_mixed = d_gated * silu_gate
    sigma = jax.nn.sigmoid(gate_pre)
    d_gate = d_gated * mixed * sigma * (1.0 + gate_pre * (1.0 - sigma))
    d_values, d_bees, d_cees, d_step_raw, g_step_bias, g_decay_log, g_skip = ssd_pull(
        d_mixed.reshape(length, heads_local, HEADDIM)
    )
    d_value_pre, g_conv_inner, g_bias_inner = inner_pull(
        d_values.reshape(length, heads_local * HEADDIM)
    )
    d_shared_pre, g_conv_shared, g_bias_shared = shared_pull(
        jnp.concatenate([d_bees, d_cees], axis=1)
    )
    d_gate_low = d_gate.astype(jnp.bfloat16)
    d_value_low = d_value_pre.astype(jnp.bfloat16)
    d_step_low = d_step_raw.astype(jnp.bfloat16)
    gate_rows, value_rows, step_rows = (
        lax.all_to_all(d_gate_low, "tensor", split_axis=0, concat_axis=1, tiled=True),
        lax.all_to_all(d_value_low, "tensor", split_axis=0, concat_axis=1, tiled=True),
        lax.all_to_all(d_step_low, "tensor", split_axis=0, concat_axis=1, tiled=True),
    )
    d_normed_own = contract_last(gate_rows, gate_all) + contract_last(value_rows, value_all)
    d_normed_own = d_normed_own + contract_last(step_rows, step_all)
    d_shared_own = sent_and_summed(d_shared_pre, "tensor", 0)
    d_shared_low = d_shared_own.astype(jnp.bfloat16)
    d_normed_own = d_normed_own + contract_last(d_shared_low, w_shared)
    shared_weight_part = contract_first(normed_own, d_shared_low)
    grad_w_gate, grad_w_value, grad_w_step, grad_w_out = side_by_side_2(
        (
            contract_first(normed, d_gate_low),
            contract_first(normed, d_value_low),
            contract_first(normed, d_step_low),
            out_weight_part,
        ),
        "dp",
        0,
        1,
    )
    d_input = d_normed_own * in_gain[None, :]
    in_gain_part = jnp.sum(d_normed_own * scaled, axis=0)
    centred = jnp.mean(d_input * scaled, axis=1, keepdims=True)
    grad_resid = inverse_in * (d_input - scaled * centred) + cotangent.astype(jnp.float32)
    (
        grad_decay_log,
        grad_skip_gain,
        grad_step_bias,
        grad_conv_inner,
        grad_bias_inner,
        grad_out_gain,
    ) = together(
        (g_decay_log, g_skip, g_step_bias, g_conv_inner, g_bias_inner, out_gain_part), "dp"
    )
    grad_w_shared, grad_in_gain, grad_conv_shared, grad_bias_shared = lax.psum(
        (shared_weight_part, in_gain_part, g_conv_shared, g_bias_shared), ("dp", "tensor")
    )
    return (
        result,
        grad_resid,
        grad_in_gain,
        grad_w_gate,
        grad_w_value,
        grad_w_step,
        grad_w_shared,
        grad_conv_inner,
        grad_bias_inner,
        grad_conv_shared,
        grad_bias_shared,
        grad_step_bias,
        grad_decay_log,
        grad_skip_gain,
        grad_out_gain,
        grad_w_out,
    )


def solution(mesh):
    in_specs = (
        P(("dp", "tensor"), None),
        P(("dp", "tensor"), None),
        P("dp"),
        P(),
        P("dp", "tensor"),
        P("dp", "tensor"),
        P("dp", "tensor"),
        P(),
        P(None, "tensor"),
        P("tensor"),
        P(),
        P(),
        P("tensor"),
        P("tensor"),
        P("tensor"),
        P("tensor"),
        P("dp", "tensor"),
    )
    out_specs = (
        P(("dp", "tensor"), None),
        P(("dp", "tensor"), None),
        P(),
        P("dp", "tensor"),
        P("dp", "tensor"),
        P("dp", "tensor"),
        P(),
        P(None, "tensor"),
        P("tensor"),
        P(),
        P(),
        P("tensor"),
        P("tensor"),
        P("tensor"),
        P("tensor"),
        P("dp", "tensor"),
    )
    return jax.shard_map(shards, mesh=mesh, in_specs=in_specs, out_specs=out_specs, check_vma=False)
```

profile of v0, /device:TPU:1, one launch (start us, length us, event | category | flops | bytes accessed | tf_op | source)
XLA Modules:
  0.0 853.0 jit_solution(17450746330004668116)
XLA Ops:
  11.5 37.2 %all_gather.19 = bf16[768,579]{1,0:T(8,128)(2,1)S(1)} all-gather(bf16[48,579]{1,0:T(8,128)(2,1)S(1)} %pad_maximum_fusion.3), channel_id=1, replica_groups=mesh['dp'=16,'tensor'=8] {'dp'}, dimensions={0}, use_global_device_ids=true | all-gather | bytes 944928 | tf_op jit(solution)/shard_map/all_gather | solution.py:18
  51.3 10.9 %all-gather.6.cloned.1.call-done = bf16[2048,768]{1,0:T(8,128)(2,1)} async-done(((bf16[256,768]{1,0:T(8,128)(2,1)}), bf16[2048,768]{1,0:T(8,128)(2,1)}) %all-gather.6.cloned.1.call-update) | async-done | bytes 3145744 | tf_op jit(solution)/shard_map/all_gather | solution.py:155
  72.1 3.9 fusion.102
  80.4 154.0 %while.46 = (s32[]{:T(128)}, f32[3,128,64]{1,2,0:T(8,128)S(1)}, s32[]{:T(128)}, f32[8,256,3,64]{1,0,3,2:T(8,128)}, f32[8,3,128,64]{2,3,1,0:T(8,128)}, /*index=5*...) while((s32[]{:T(128)}, f32[3,128,64]{1,2,0:T(8,128)S(1)}, ...), condition=%wide.region_4.5_spmd.clone, body=%wide.region_1.4_spmd.clone.sunk | while | flops 404155904 | bytes 3612777 | solution.py:110
  90.2 5.5 dynamic_update_slice.90
  109.5 5.5 dynamic_update_slice.90
  128.7 5.5 dynamic_update_slice.90
  148.0 5.5 dynamic_update_slice.90
  167.2 5.5 dynamic_update_slice.90
  186.5 5.5 dynamic_update_slice.90
  205.7 5.5 dynamic_update_slice.90
  224.9 5.5 dynamic_update_slice.90
  236.7 5.3 multiply_reduce_fusion.16
  242.1 8.4 all_to_all.97
  250.5 5.5 multiply_reduce_fusion.9
  265.2 5.8 multiply_reduce_fusion.14
  277.5 268.6 %while.47 = (s32[]{:T(128)}, f32[3,128,64]{1,2,0:T(8,128)S(1)}, f32[8,256,3,64]{1,0,3,2:T(8,128)}, f32[8,256,128]{2,1,0:T(8,128)}, f32[8,256,128]{2,1,0:T(8,128)...) while((s32[]{:T(128)}, f32[3,128,64]{1,2,0:T(8,128)S(1)}, ...), condition=%wide.region_21.22_spmd.clone, body=%wide.region_9.21_spmd.clone.sunk | while | flops 986370560 | bytes 13397370 | solution.py:110
  298.5 3.8 reduce-window.74
  305.2 5.5 dynamic_update_slice.96
  332.1 3.8 reduce-window.74
  338.8 5.5 dynamic_update_slice.96
  365.7 3.8 reduce-window.74
  372.4 5.5 dynamic_update_slice.96
  399.2 3.8 reduce-window.74
  406.0 5.5 dynamic_update_slice.96
  432.8 3.8 reduce-window.74
  439.6 5.5 dynamic_update_slice.96
  466.4 3.8 reduce-window.74
  473.1 5.5 dynamic_update_slice.96
  500.0 3.8 reduce-window.74
  506.7 5.5 dynamic_update_slice.96
  533.6 3.8 reduce-window.74
  540.3 5.5 dynamic_update_slice.96
  551.0 4.0 all-to-all-start.5
  555.0 6.9 fusion.127
  568.4 3.8 fusion.126
  578.1 10.3 %all-to-all-start.7 = ((f32[16,1,1161]{2,1,0:T(1,128)}), f32[16,1,1161]{2,1,0:T(1,128)S(1)}, u32[]{:S(2)}, u32[]{:S(2)}) async-start(f32[16,1,1161]{2,1,0:T(1,128)} %broadcast_in_dim.365), calls=%async_computation.7 | async-start | bytes 163840 | tf_op jit(solution)/shard_map/all_to_all | solution.py:27
  595.8 4.8 all-to-all-start.1
  600.6 3.6 fusion.146
  604.3 4.1 multiply_add_fusion
  608.4 3.9 all-to-all-done.1
  612.3 4.2 all-to-all-start.6
  625.0 35.1 %all-gather = bf16[8,3,768]{2,1,0:T(4,128)(2,1)S(1)} all-gather(bf16[1,3,768]{2,1,0:T(4,128)(2,1)} %copy.235), channel_id=1, replica_groups=mesh['dp'=16,'tensor'=8] {'tensor'}, dimensions={0}, use_global_device_ids=true | all-gather | bytes 41472 | tf_op jit(solution)/shard_map/all_gather | solution.py:196
  664.7 4.2 all-to-all-start.4
  677.3 3.5 all-to-all-start.3
  683.6 3.6 fusion.78
  693.4 71.9 %all-reduce.24 = (f32[768]{0:T(1024)}, f32[4,256]{1,0:T(4,128)}, f32[256]{0:T(256)}) all-reduce(f32[768]{0:T(1024)S(1)} %get-tuple-element.965, f32[4,256]{1,0:T(4,128)S(1)} %copy-done.42, f32[256]{0:T(256)S(1)} %copy-done.64), channel_id=1, replica_groups=mesh['dp'=16,'tensor'=8] {'dp','tensor'}, use_global_device_ids=true, to_apply=%region_25.26 | all-reduce | flops 2048 | bytes 16384 | tf_op jit(solution)/shard_map/psum | solution.py:260
  769.4 74.2 %all-reduce.27.cloned.1.call-done = f32[768,256]{1,0:T(8,128)} async-done(((f32[768,256]{1,0:T(8,128)}), f32[768,256]{1,0:T(8,128)}) %all-reduce.27.cloned.1.call-update) | async-done | bytes 786448 | tf_op jit(solution)/shard_map/psum | solution.py:260
  (912 shorter events, 381.5 us)
Async XLA Ops:
  7.2 63.1 %copy-start = (bf16[768,256]{1,0:T(8,128)(2,1)S(1)}, bf16[768,256]{1,0:T(8,128)(2,1)}, u32[]{:S(2)}) copy-start(bf16[768,256]{1,0:T(8,128)(2,1)} %param.28) | copy-start | bytes 1179652
  7.2 4.2 copy-start.37
  7.2 4.2 copy-start.36
  7.2 54.9 %all-gather.6.cloned.1.call-start = ((), (), s32[]{:S(2)}) async-start(), calls=%async_computation.9 | async-start | bytes 3538944 | tf_op jit(solution)/shard_map/all_gather | solution.py:155
  10.4 240.1 %all-gather.10.cloned.1.call-start = ((), (), s32[]{:S(2)}) async-start(), calls=%async_computation.11 | async-start | bytes 3538944 | tf_op jit(solution)/shard_map/all_gather | solution.py:202
  11.2 659.0 %all-gather.8.cloned.1.call-start = ((), (), s32[]{:S(2)}) async-start(), calls=%async_computation.10 | async-start | bytes 2654208 | tf_op jit(solution)/shard_map/all_gather | solution.py:197
  48.7 28.9 %copy-start.9 = (bf16[768,579]{1,0:T(8,128)(2,1)}, bf16[768,579]{1,0:T(8,128)(2,1)S(1)}, u32[]{:S(2)}) copy-start(bf16[768,579]{1,0:T(8,128)(2,1)S(1)} %all_gather.19) | copy-start | bytes 2668036
  50.9 14.4 %copy-start.43 = (f32[1,192]{1,0:T(1,128)}, f32[1,192]{1,0:T(1,128)S(1)}, u32[]{:S(2)}) copy-start(f32[1,192]{1,0:T(1,128)S(1)} %get-tuple-element.1087) | copy-start | bytes 2308
  50.9 14.4 %copy-start.45 = (f32[1,192]{1,0:T(1,128)}, f32[1,192]{1,0:T(1,128)S(1)}, u32[]{:S(2)}) copy-start(f32[1,192]{1,0:T(1,128)S(1)} %get-tuple-element.1088) | copy-start | bytes 2308
  50.9 14.4 %copy-start.47 = (f32[1,192]{1,0:T(1,128)}, f32[1,192]{1,0:T(1,128)S(1)}, u32[]{:S(2)}) copy-start(f32[1,192]{1,0:T(1,128)S(1)} %get-tuple-element.1089) | copy-start | bytes 2308
  50.9 14.4 %copy-start.59 = (f32[1,192]{1,0:T(1,128)}, f32[1,192]{1,0:T(1,128)S(1)}, u32[]{:S(2)}) copy-start(f32[1,192]{1,0:T(1,128)S(1)} %get-tuple-element.1086) | copy-start | bytes 2308
  50.9 21.1 %copy-start.51 = (f32[1,256]{1,0:T(1,128)}, f32[1,256]{1,0:T(1,128)S(1)}, u32[]{:S(2)}) copy-start(f32[1,256]{1,0:T(1,128)S(1)} %get-tuple-element.1083) | copy-start | bytes 3076
  51.0 21.1 %copy-start.53 = (f32[1,256]{1,0:T(1,128)}, f32[1,256]{1,0:T(1,128)S(1)}, u32[]{:S(2)}) copy-start(f32[1,256]{1,0:T(1,128)S(1)} %get-tuple-element.1084) | copy-start | bytes 3076
  51.0 21.1 %copy-start.55 = (f32[1,256]{1,0:T(1,128)}, f32[1,256]{1,0:T(1,128)S(1)}, u32[]{:S(2)}) copy-start(f32[1,256]{1,0:T(1,128)S(1)} %get-tuple-element.1085) | copy-start | bytes 3076
  51.0 21.1 %copy-start.57 = (f32[1,256]{1,0:T(1,128)}, f32[1,256]{1,0:T(1,128)S(1)}, u32[]{:S(2)}) copy-start(f32[1,256]{1,0:T(1,128)S(1)} %get-tuple-element.1082) | copy-start | bytes 3076
  51.0 26.5 %copy-start.71 = (f32[3]{0:T(128)}, f32[3]{0:T(128)S(1)}, u32[]{:S(2)}) copy-start(f32[3]{0:T(128)S(1)} %exponential_negate_fusion) | copy-start | bytes 40
  51.2 214.0 %copy-start.49 = (f32[192]{0:T(256)}, f32[192]{0:T(256)S(1)}, u32[]{:S(2)}) copy-start(f32[192]{0:T(256)S(1)} %mul.689) | copy-start | bytes 2308
  51.3 14.1 %copy-start.73 = (f32[192]{0:T(256)S(1)}, f32[192]{0:T(256)}, u32[]{:S(2)}) copy-start(f32[192]{0:T(256)} %param.30) | copy-start | bytes 2308
  236.5 5.5 copy-start.17
  236.7 13.8 %copy-start.61 = (f32[192]{0:T(256)S(1)}, f32[192]{0:T(256)}, u32[]{:S(2)}) copy-start(f32[192]{0:T(256)} %param.36) | copy-start | bytes 2308
  256.7 8.5 all-to-all-start.2
  260.0 423.6 %all-gather.12.cloned.1.call-start = ((), (), s32[]{:S(2)}) async-start(), calls=%async_computation.12 | async-start | bytes 5308416 | tf_op jit(solution)/shard_map/all_gather | solution.py:18
  294.5 8.7 %copy-start.16 = (f32[256,256]{1,0:T(8,128)S(1)}, f32[256,256]{1,0:T(8,128)}, u32[]{:S(2)}) copy-start(f32[256,256]{1,0:T(8,128)} %copy-done.15) | copy-start | bytes 786436 | tf_op jit(solution)/shard_map/transpose(jvp())/while
  328.1 8.7 %copy-start.16 = (f32[256,256]{1,0:T(8,128)S(1)}, f32[256,256]{1,0:T(8,128)}, u32[]{:S(2)}) copy-start(f32[256,256]{1,0:T(8,128)} %copy-done.15) | copy-start | bytes 786436 | tf_op jit(solution)/shard_map/transpose(jvp())/while
  361.7 8.7 %copy-start.16 = (f32[256,256]{1,0:T(8,128)S(1)}, f32[256,256]{1,0:T(8,128)}, u32[]{:S(2)}) copy-start(f32[256,256]{1,0:T(8,128)} %copy-done.15) | copy-start | bytes 786436 | tf_op jit(solution)/shard_map/transpose(jvp())/while
  395.3 8.7 %copy-start.16 = (f32[256,256]{1,0:T(8,128)S(1)}, f32[256,256]{1,0:T(8,128)}, u32[]{:S(2)}) copy-start(f32[256,256]{1,0:T(8,128)} %copy-done.15) | copy-start | bytes 786436 | tf_op jit(solution)/shard_map/transpose(jvp())/while
  428.8 8.7 %copy-start.16 = (f32[256,256]{1,0:T(8,128)S(1)}, f32[256,256]{1,0:T(8,128)}, u32[]{:S(2)}) copy-start(f32[256,256]{1,0:T(8,128)} %copy-done.15) | copy-start | bytes 786436 | tf_op jit(solution)/shard_map/transpose(jvp())/while
  462.4 8.7 %copy-start.16 = (f32[256,256]{1,0:T(8,128)S(1)}, f32[256,256]{1,0:T(8,128)}, u32[]{:S(2)}) copy-start(f32[256,256]{1,0:T(8,128)} %copy-done.15) | copy-start | bytes 786436 | tf_op jit(solution)/shard_map/transpose(jvp())/while
  496.0 8.7 %copy-start.16 = (f32[256,256]{1,0:T(8,128)S(1)}, f32[256,256]{1,0:T(8,128)}, u32[]{:S(2)}) copy-start(f32[256,256]{1,0:T(8,128)} %copy-done.15) | copy-start | bytes 786436 | tf_op jit(solution)/shard_map/transpose(jvp())/while
  529.6 8.7 %copy-start.16 = (f32[256,256]{1,0:T(8,128)S(1)}, f32[256,256]{1,0:T(8,128)}, u32[]{:S(2)}) copy-start(f32[256,256]{1,0:T(8,128)} %copy-done.15) | copy-start | bytes 786436 | tf_op jit(solution)/shard_map/transpose(jvp())/while
  546.2 8.8 %copy-start.79 = (f32[3]{0:T(128)S(1)}, f32[3]{0:T(128)}, u32[]{:S(2)}) copy-start(f32[3]{0:T(128)} %param.34) | copy-start | bytes 40
  546.2 8.8 %copy-start.50 = (f32[192]{0:T(256)S(1)}, f32[192]{0:T(256)}, u32[]{:S(2)}) copy-start(f32[192]{0:T(256)} %copy-done.49) | copy-start | bytes 2308
  551.0 26.5 %all-to-all-start.5 = ((bf16[8,256,3]{1,2,0:T(4,128)(2,1)}), bf16[8,256,3]{1,2,0:T(4,128)(2,1)S(1)}, u32[]{:S(2)}, u32[]{:S(2)}) async-start(bf16[8,256,3]{1,2,0:T(4,128)(2,1)} %bitcast.25), calls=%async_computation.5 | async-start | bytes 32768 | tf_op jit(solution)/shard_map/all_to_all | solution.py:227
  555.0 6.9 copy-start.39
  555.0 6.9 copy-start.48
  575.5 13.0 %copy-start.13 = (bf16[2048,192]{0,1:T(8,128)(2,1)S(1)}, bf16[2048,192]{0,1:T(8,128)(2,1)}, u32[]{:S(2)}) copy-start(bf16[2048,192]{0,1:T(8,128)(2,1)} %get-tuple-element.1064) | copy-start | bytes 2359300
  577.4 14.5 %copy-start.32 = (bf16[8,256,3]{1,2,0:T(4,128)(2,1)}, bf16[8,256,3]{1,2,0:T(4,128)(2,1)S(1)}, u32[]{:S(2)}) copy-start(bf16[8,256,3]{1,2,0:T(4,128)(2,1)S(1)} %all-to-all-done.5) | copy-start | bytes 36868
  578.1 17.7 %all-to-all-start.7 = ((f32[16,1,1161]{2,1,0:T(1,128)}), f32[16,1,1161]{2,1,0:T(1,128)S(1)}, u32[]{:S(2)}, u32[]{:S(2)}) async-start(f32[16,1,1161]{2,1,0:T(1,128)} %broadcast_in_dim.365), calls=%async_computation.7 | async-start | bytes 163840 | tf_op jit(solution)/shard_map/all_to_all | solution.py:27
  592.0 8.6 %copy-start.12 = (bf16[2048,192]{0,1:T(8,128)(2,1)S(1)}, bf16[2048,192]{0,1:T(8,128)(2,1)}, u32[]{:S(2)}) copy-start(bf16[2048,192]{0,1:T(8,128)(2,1)} %get-tuple-element.1061) | copy-start | bytes 2359300
  595.8 16.5 %all-to-all-start.1 = ((bf16[8,256,192]{1,2,0:T(8,128)(2,1)}), bf16[8,256,192]{1,2,0:T(8,128)(2,1)}, u32[]{:S(2)}, u32[]{:S(2)}) async-start(bf16[8,256,192]{1,2,0:T(8,128)(2,1)} %bitcast.302), calls=%async_computation.1 | async-start | bytes 1572864 | tf_op jit(solution)/shard_map/all_to_all | solution.py:199
  612.3 52.4 %all-to-all-start.6 = ((f32[8,256,256]{2,1,0:T(8,128)}), f32[8,256,256]{2,1,0:T(8,128)S(1)}, u32[]{:S(2)}, u32[]{:S(2)}) async-start(f32[8,256,256]{2,1,0:T(8,128)} %bitcast.479), calls=%async_computation.6 | async-start | bytes 4194304 | tf_op jit(solution)/shard_map/all_to_all | solution.py:44
  616.5 149.9 %reduce-scatter.4.cloned.1.call-start = ((), (), s32[]{:S(2)}) async-start(), calls=%async_computation.14 | async-start | bytes 2088960
  663.3 6.9 copy-start.18
  664.7 12.6 %all-to-all-start.4 = ((bf16[8,256,192]{1,2,0:T(8,128)(2,1)}), bf16[8,256,192]{1,2,0:T(8,128)(2,1)}, u32[]{:S(2)}, u32[]{:S(2)}) async-start(bf16[8,256,192]{1,2,0:T(8,128)(2,1)} %bitcast.496), calls=%async_computation.4 | async-start | bytes 1572864 | tf_op jit(solution)/shard_map/all_to_all | solution.py:226
  673.7 7.5 copy-start.21
  677.3 12.6 %all-to-all-start.3 = ((bf16[8,256,192]{1,2,0:T(8,128)(2,1)}), bf16[8,256,192]{1,2,0:T(8,128)(2,1)S(1)}, u32[]{:S(2)}, u32[]{:S(2)}) async-start(bf16[8,256,192]{1,2,0:T(8,128)(2,1)} %bitcast.495), calls=%async_computation.3 | async-start | bytes 1572864 | tf_op jit(solution)/shard_map/all_to_all | solution.py:225
  680.8 162.7 %all-reduce.27.cloned.1.call-start = ((), (), s32[]{:S(2)}) async-start(), calls=%async_computation.13 | async-start | bytes 1572864 | tf_op jit(solution)/shard_map/psum | solution.py:260
  692.7 72.6 %copy-start.28 = (bf16[256,768]{1,0:T(8,128)(2,1)S(1)}, bf16[256,768]{1,0:T(8,128)(2,1)}, u32[]{:S(2)}) copy-start(bf16[256,768]{1,0:T(8,128)(2,1)} %param.22) | copy-start | bytes 1179652
  (73 other events, 183.0 us)
Sparse Core Ops, SparseCore 0:
  10.6 51.5 all-gather.5
  63.8 41.9 all-gather.9
  107.4 39.5 all-gather.7
  262.5 61.1 all-gather.11
  623.5 68.9 reduce-scatter.3
  697.0 146.5 all-reduce.26
where the time goes:
time: 864 us; the launch traced here: 853 us
  local copies, waits for them, and re-layouts  225 us (26%)
  matrix products  172 us (20%)
  blocking collectives  153 us (18%)
  other arithmetic  131 us (15%)
  waiting for transfers between devices  100 us (12%)
  starting transfers between devices  34.9 us (4%)
  loops' own time  22.6 us (3%)
  between operations  15.6 us (2%)
    dynamic_update_slice x48, local copies, waits for them, and re-layouts, block_scan(): lax.scan(jax.checkpoint(advance), start, (split(values), split(bees), spl...  106 us
    psum x1, waiting for transfers between devices, shards(): lax.psum((shared_weight_part, in_gain_part, g_conv_shared, g_bias_shared)...  74.2 us
    psum x1, blocking collectives, shards(): lax.psum((shared_weight_part, in_gain_part, g_conv_shared, g_bias_shared)...  71.9 us
    dot_general x24, matrix products, advance(): inside = jnp.einsum('hts,shp->thp', mixing, vals, precision=HIGHEST)  46.9 us
    another operation x49, other arithmetic  45.7 us
    dot_general x32, matrix products, advance(): scores = jnp.dot(cmat, bmat.T, precision=HIGHEST)  40.1 us
    all_gather x1, blocking collectives, side_by_side(): lax.all_gather(both, axis, axis=dim, tiled=True)  37.2 us
    all_gather x1, blocking collectives, shards(): lax.all_gather(full_step, 'tensor', axis=1, tiled=True)  35.1 us
  transfers between devices with their start and end apart: 13, of which 7 were waited for; matrix products, arithmetic and copies ran while one was open for 61% of the time, Pallas kernels for 0%

commit v1 on v0

v1 whole, which is shorter than its diff:
```python
import jax
import jax.numpy as jnp
from jax import lax
from jax.experimental import pallas as pl
from jax.experimental.pallas import tpu as pltpu
from jax.sharding import PartitionSpec as P

D = 768
HEADS = 24
HEADDIM = 64
STATE = 128
INNER = 1536
ROWS = 256
HALO = 16
PARTS = 8
WIDE = 192
PACK = 640
EPSILON = 1e-05
VMEM_LIMIT = 60 * 1024 * 1024
MESH = pl.DeviceIdType.MESH
HIGHEST = lax.Precision.HIGHEST
F32 = jnp.float32
BF16 = jnp.bfloat16

ORDERS = (("x", "y", "z"), ("y", "z", "x"), ("z", "x", "y"))
DIMS = ("x", "y", "z")


def place():
    dp, tensor = lax.axis_index("dp"), lax.axis_index("tensor")
    x = (dp // 2 % 2) * 2 + tensor // 4
    return {"x": x, "y": tensor % 4, "z": dp // 4, "core": dp % 2}


def device_of(at):
    return (at["z"] * 4 + (at["x"] // 2) * 2 + at["core"], (at["x"] % 2) * 4 + at["y"])


def moved(me, dim, by):
    return {**me, dim: (me[dim] + by) % 4}


def sibling(me):
    return {**me, "core": 1 - me["core"]}


def region(fixed):
    free = slice(None)
    x_lo, x_hi = (fixed["x"] % 2, fixed["x"] // 2) if "x" in fixed else (free, free)
    return (x_lo, fixed.get("y", free), fixed.get("z", free), x_hi)


def free_shape(fixed):
    sizes = (("x", 2), ("y", 4), ("z", 4), ("x", 2))
    return tuple(size for dim, size in sizes if dim not in fixed)


def greet(me):
    barrier = pltpu.get_barrier_semaphore()
    others = [moved(me, dim, by) for dim in DIMS for by in (1, 2, 3)] + [sibling(me)]
    for other in others:
        pl.semaphore_signal(barrier, inc=1, device_id=device_of(other), device_id_type=MESH)
    pl.semaphore_wait(barrier, len(others))


def send(src, dst, sems, slot, target):
    send_sem, recv_sem = sems
    copy = pltpu.make_async_remote_copy(
        src_ref=src,
        dst_ref=dst,
        send_sem=send_sem.at[slot],
        recv_sem=recv_sem.at[slot],
        device_id=device_of(target),
        device_id_type=MESH,
    )
    copy.start()
    return copy


def spread(me, own, buf, sems, base):
    core = me["core"]
    pending = []

    def part(p, dims):
        return buf.at[region({dim: me[dim] for dim in dims}) + (core, p)]

    def along(p, stage, src, dst):
        dim = ORDERS[p][stage]
        return [
            send(src, dst, sems, base + p * 13 + stage * 3 + by - 1, moved(me, dim, by))
            for by in (1, 3, 2)
        ]

    def across(p, value, step):
        piece = buf.at[region({ORDERS[p][2]: value}) + (core, p)]
        pending.append(send(piece, piece, sems, base + p * 13 + 9 + step, sibling(me)))

    started = [along(p, 0, own(p), part(p, ORDERS[p])) for p in range(3)]
    for stage in (1, 2):
        following = []
        for p in range(3):
            for copy in started[p]:
                copy.wait_recv()
            pending.extend(started[p])
            piece = part(p, ORDERS[p][stage:])
            following.append((along(p, stage, piece, piece)))
        for p in range(3):
            for copy in started[p]:
                copy.wait_send()
        pending = [copy for copy in pending if all(copy is not c for s in started for c in s)]
        started = following
    for p in range(3):
        across(p, me[ORDERS[p][2]], 0)
    for order, by in enumerate((1, 3, 2)):
        for p in range(3):
            started[p][order].wait_recv()
            across(p, (me[ORDERS[p][2]] - by) % 4, by)
    for p in range(3):
        for copy in started[p]:
            copy.wait_send()
    for copy in pending:
        copy.wait()


GATHER_SEMS = 39


def gather_kernel(w_ref, out_ref, send_sem, recv_sem, local_sem):
    me = place()
    greet(me)
    here = region({dim: me[dim] for dim in DIMS}) + (me["core"],)
    keep = pltpu.make_async_copy(w_ref, out_ref.at[here], local_sem)
    keep.start()
    keep.wait()
    spread(me, lambda p: w_ref.at[p], out_ref, (send_sem, recv_sem), 0)


def gather_weights(block):
    out = pl.pallas_call(
        gather_kernel,
        out_shape=jax.ShapeDtypeStruct((2, 4, 4, 2, 2, 3, 16, PACK), BF16),
        in_specs=[pl.BlockSpec(memory_space=pl.ANY)],
        out_specs=pl.BlockSpec(memory_space=pl.ANY),
        scratch_shapes=[
            pltpu.SemaphoreType.DMA((GATHER_SEMS,)),
            pltpu.SemaphoreType.DMA((GATHER_SEMS,)),
            pltpu.SemaphoreType.DMA,
        ],
        compiler_params=pltpu.CompilerParams(collective_id=0, has_side_effects=True),
    )(block.reshape(3, 16, PACK))
    return out.reshape(PARTS, D, PACK)


TAIL = 128


def reduce_kernel(
    part_ref, small_ref, out_ref, tail_ref, small_out,
    own, heard, got_c, got_b, got_a, sum_c, sum_b, tail, small_got, small_sum,
    send_sem, recv_sem, small_send, small_recv, local_sem, tail_send, tail_recv,
):
    me = place()
    core = me["core"]
    greet(me)
    sems = (send_sem, recv_sem)
    small_sems = (small_send, small_recv)
    steps = (1, 3, 2, 0)
    copies = {}
    waiting = []

    def last(p, by):
        dim = ORDERS[p][2]
        return {dim: (me[dim] + by) % 4}

    for by in steps:
        for p in range(3):
            there = region(last(p, by))
            copies[p, by] = (
                send(part_ref.at[there + (1 - core, p)], heard[p].at[by], sems, p * 13 + by, sibling(me)),
                pltpu.make_async_copy(part_ref.at[there + (core, p)], own[p].at[by], local_sem.at[p * 4 + by]),
            )
            copies[p, by][1].start()
    small_copy = send(small_ref, small_got.at[9], small_sems, 9, sibling(me))

    onward = {}
    for by in steps:
        for p in range(3):
            remote, local = copies[p, by]
            local.wait()
            remote.wait_recv()
            own[p][by] = own[p][by] + heard[p][by]
            if by:
                onward[p, by] = send(
                    own[p].at[by], got_c[p].at[by - 1], sems, p * 13 + 4 + by - 1, moved(me, ORDERS[p][2], by)
                )
    small_copy.wait()
    small_sum[0] = small_ref[...] + small_got[9]

    def small_send_along(stage, dim):
        return [
            send(small_sum.at[stage], small_got.at[stage * 3 + by - 1], small_sems, stage * 3 + by - 1, moved(me, dim, by))
            for by in (1, 3, 2)
        ]

    def small_add(stage, sent):
        for copy in sent:
            copy.wait_recv()
        waiting.extend(sent)
        base = stage * 3
        total = (small_sum[stage] + small_got[base]) + (small_got[base + 1] + small_got[base + 2])
        if stage < 2:
            small_sum[stage + 1] = total
        else:
            small_out[...] = total

    small_sent = small_send_along(0, "z")
    for p in range(3):
        for by in (1, 3, 2):
            onward[p, by].wait_recv()
        got = got_c[p]
        sum_c[p][...] = (
            (own[p][0].astype(F32) + got[0].astype(F32)) + (got[1].astype(F32) + got[2].astype(F32))
        ).astype(BF16)
    small_add(0, small_sent)
    small_sent = small_send_along(1, "y")

    second = {}
    for p in range(3):
        dim, fixed = ORDERS[p][1], ORDERS[p][2]
        for by in (1, 3, 2):
            second[p, by] = send(
                sum_c[p].at[inner_index(p, dim, (me[dim] + by) % 4)],
                got_b[p].at[by - 1], sems, p * 13 + 7 + by - 1, moved(me, dim, by),
            )
    for p in range(3):
        dim = ORDERS[p][1]
        for by in (1, 3, 2):
            second[p, by].wait_recv()
        got = got_b[p]
        mine = sum_c[p][inner_index(p, dim, me[dim])]
        sum_b[p][...] = (
            (mine.astype(F32) + got[0].astype(F32)) + (got[1].astype(F32) + got[2].astype(F32))
        ).astype(BF16)
    small_add(1, small_sent)
    small_sent = small_send_along(2, "x")

    third = {}
    for p in range(3):
        dim = ORDERS[p][0]
        for by in (1, 3, 2):
            third[p, by] = send(
                sum_b[p].at[line_index(p, dim, (me[dim] + by) % 4)],
                got_a.at[p, by - 1], sems, p * 13 + 10 + by - 1, moved(me, dim, by),
            )
    for p in range(3):
        dim = ORDERS[p][0]
        for by in (1, 3, 2):
            third[p, by].wait_recv()
        mine = sum_b[p][line_index(p, dim, me[dim])].astype(F32)
        total = (mine + got_a[p, 0].astype(F32)) + (got_a[p, 1].astype(F32) + got_a[p, 2].astype(F32))
        out_ref[p] = total
        tail[p] = total[:, PACK - TAIL:].astype(BF16)
    small_add(2, small_sent)

    here = region({dim: me[dim] for dim in DIMS}) + (core,)
    keep = pltpu.make_async_copy(tail, tail_ref.at[here], local_sem.at[12])
    keep.start()
    keep.wait()
    spread(me, lambda p: tail.at[p], tail_ref, (tail_send, tail_recv), 0)

    for remote, local in copies.values():
        remote.wait_send()
    for copy in list(onward.values()) + list(second.values()) + list(third.values()) + waiting:
        copy.wait_send()


def inner_index(p, dim, value):
    full = region({dim: value})
    fixed = ORDERS[p][2]
    return tuple(i for i, name in zip(full, ("x", "y", "z", "x")) if name != fixed)


def line_index(p, dim, value):
    full = region({dim: value})
    return tuple(i for i, name in zip(full, ("x", "y", "z", "x")) if name == dim)


def reduce_grads(parts, small):
    big = parts.reshape(2, 4, 4, 2, 2, 3, 16, PACK)
    block = (16, PACK)

    def shapes(lead, stage):
        return [pltpu.VMEM(lead + free_shape(ORDERS[p][stage:]) + block, BF16) for p in range(3)]

    def body(part_ref, small_ref, out_ref, tail_ref, small_out, *rest):
        groups = [rest[i * 3 : i * 3 + 3] for i in range(2)]
        rest = rest[6:]
        got_c, rest = rest[:3], rest[3:]
        got_b, rest = rest[:3], rest[3:]
        got_a, rest = rest[0], rest[1:]
        sum_c, rest = rest[:3], rest[3:]
        sum_b, rest = rest[:3], rest[3:]
        reduce_kernel(part_ref, small_ref, out_ref, tail_ref, small_out, groups[0], groups[1], got_c, got_b, got_a, sum_c, sum_b, *rest)

    rows = small.shape[0]
    dma = pltpu.SemaphoreType.DMA
    out, tail, total = pl.pallas_call(
        body,
        out_shape=(
            jax.ShapeDtypeStruct((3, 16, PACK), F32),
            jax.ShapeDtypeStruct((2, 4, 4, 2, 2, 3, 16, TAIL), BF16),
            jax.ShapeDtypeStruct((rows, 128), F32),
        ),
        in_specs=[pl.BlockSpec(memory_space=pl.ANY), pl.BlockSpec(memory_space=pltpu.VMEM)],
        out_specs=(
            pl.BlockSpec(memory_space=pltpu.VMEM),
            pl.BlockSpec(memory_space=pl.ANY),
            pl.BlockSpec(memory_space=pltpu.VMEM),
        ),
        scratch_shapes=[
            *shapes((4,), 2), *shapes((4,), 2), *shapes((3,), 2), *shapes((3,), 1),
            pltpu.VMEM((3, 3) + block, BF16),
            *shapes((), 2), *shapes((), 1),
            pltpu.VMEM((3, 16, TAIL), BF16),
            pltpu.VMEM((10, rows, 128), F32),
            pltpu.VMEM((3, rows, 128), F32),
            dma((39,)), dma((39,)), dma((10,)), dma((10,)), dma((13,)),
            dma((GATHER_SEMS,)), dma((GATHER_SEMS,)),
        ],
        compiler_params=pltpu.CompilerParams(
            collective_id=1, has_side_effects=True, vmem_limit_bytes=VMEM_LIMIT
        ),
    )(big, small)
    return out.reshape(48, PACK), tail.reshape(PARTS, D, TAIL), total


def dot(a, b, over_a, over_b, precision=None):
    return lax.dot_general(
        a, b, (((over_a,), (over_b,)), ((), ())), precision=precision, preferred_element_type=F32
    )


def head_lanes():
    head = lax.broadcasted_iota(jnp.int32, (128, INNER), 0)
    unit = lax.broadcasted_iota(jnp.int32, (128, INNER), 1)
    return jnp.where(unit // HEADDIM == head, 1.0, 0.0).astype(BF16)


def halves(v):
    top = v.astype(BF16)
    return top, (v - top.astype(F32)).astype(BF16)


def to_units(v, spread_heads):
    top, rest = halves(v)
    return dot(top, spread_heads, 1, 0) + dot(rest, spread_heads, 1, 0)


def to_heads(v, spread_heads):
    top, rest = halves(v)
    return dot(top, spread_heads, 1, 1) + dot(rest, spread_heads, 1, 1)


def lower_triangle():
    row = lax.broadcasted_iota(jnp.int32, (ROWS, ROWS), 0)
    return row >= lax.broadcasted_iota(jnp.int32, (ROWS, ROWS), 1)


def conv_sum(before, taps, bias, same):
    total = bias + taps[3:4] * before[HALO:]
    for back in (1, 2, 3):
        total = total + taps[3 - back : 4 - back] * (same[:, back : back + 1] * before[HALO - back : HALO - back + ROWS])
    return total


def silu_slope(v):
    sig = jax.nn.sigmoid(v)
    return sig * (1.0 + v * (1.0 - sig))


def step_weights(w_ref):
    total = w_ref[0, :, PACK - 128 :]
    for t in range(1, PARTS):
        total = total + w_ref[t, :, PACK - 128 :]
    return total


def enter_kernel(
    x_ref, gain_ref, w_ref, wsh_ref, prm_ref, hp_ref, csh_ref, bsh_ref, same_ref, ends_ref,
    normed_ref, gate_ref, vpre_ref, vsum_ref, val_ref, spre_ref, ssum_ref, bc_ref,
    raw_ref, dt_ref, logs_ref, fresh_ref,
):
    x = x_ref[...].astype(F32)
    inverse = lax.rsqrt(jnp.mean(x * x, axis=1, keepdims=True) + EPSILON)
    normed = (x * inverse * gain_ref[...]).astype(BF16)
    normed_ref[...] = normed[HALO:]
    same = same_ref[...]
    for t in range(PARTS):
        cols = slice(t * WIDE, (t + 1) * WIDE)
        both = dot(normed, w_ref[t, :, : 2 * WIDE], 1, 0)
        gate_ref[:, cols] = both[HALO:, :WIDE]
        before = both[:, WIDE:]
        vpre_ref[:, cols] = before
        total = conv_sum(before, prm_ref[0:4, cols], prm_ref[4:5, cols], same)
        vsum_ref[:, cols] = total
        val_ref[:, cols] = (total * jax.nn.sigmoid(total)).astype(BF16)
    before = dot(normed, wsh_ref[...], 1, 0)
    spre_ref[...] = before
    total = conv_sum(before, csh_ref[...], bsh_ref[...], same)
    ssum_ref[...] = total
    bc_ref[...] = (total * jax.nn.sigmoid(total)).astype(BF16)

    step = dot(normed[HALO:], step_weights(w_ref), 1, 0)
    is_head = lax.broadcasted_iota(jnp.int32, (ROWS, 128), 1) < HEADS
    raw = jnp.where(is_head, pltpu.roll(step, 64, 1) + hp_ref[0:1], 0.0)
    raw_ref[...] = raw
    dt = jnp.where(is_head, jnp.maximum(raw, 0.0) + jnp.log1p(jnp.exp(-jnp.abs(raw))), 0.0)
    dt_ref[...] = dt
    logs = dot(lower_triangle().astype(F32), dt * hp_ref[1:2], 1, 0, HIGHEST)
    logs_ref[...] = logs
    lanes = head_lanes()
    last = logs[ROWS - 1 :]
    ends = ends_ref[...]
    weights = ends[:, 0:1] * jnp.exp(last - logs) * dt
    weighted = (val_ref[...].astype(F32) * to_units(weights, lanes)).astype(BF16)
    fresh_ref[0:STATE] = dot(bc_ref[:, :STATE], weighted, 0, 0).astype(BF16)
    kept = to_units(ends[0:8, 2:3] * jnp.exp(jnp.broadcast_to(last, (8, 128))), lanes)
    top, rest = halves(kept[0:1])
    row = lax.broadcasted_iota(jnp.int32, (16, INNER), 0)
    fresh_ref[STATE:] = jnp.where(row == 0, top.astype(F32), jnp.where(row == 1, rest.astype(F32), 0.0)).astype(BF16)


def middle_kernel(
    x_ref, cot_ref, w_ref, prm_ref, hp_ref, gate_ref, val_ref, bc_ref, dt_ref, logs_ref,
    state_ref, ends_ref, ids_ref,
    result_ref, nout_ref, dgate_ref, dval_ref, dscore_ref, dstate_ref, dlog_ref, direct_ref, rows_ref,
    mix_ref, dec_ref, mixed_ref, inner_ref, dout_ref, dy_ref,
):
    lanes = head_lanes()
    ends = ends_ref[...]
    logs, dt = logs_ref[...], dt_ref[...]
    logs_t, dt_t = logs.T, dt.T
    bmat, cmat = bc_ref[:, :STATE], bc_ref[:, STATE:]
    allowed = lower_triangle() & (ends[:, 3:4] == ids_ref[...])
    scores = jnp.where(allowed, dot(cmat, bmat, 1, 1), 0.0)
    carried = to_units(ends[:, 1:2] * jnp.exp(logs), lanes)
    state = state_ref[...]
    inner_ref[...] = dot(cmat, state, 1, 0) * carried
    first_half = lax.broadcasted_iota(jnp.int32, (ROWS, 128), 1) < HEADDIM

    def pair(ref, tile):
        both = ref[:, tile * 128 : tile * 128 + 128]
        zero = jnp.zeros_like(both)
        return jnp.where(first_half, both, zero), jnp.where(first_half, zero, both)

    for tile in range(HEADS // 2):
        cols = slice(tile * 128, tile * 128 + 128)
        total = inner_ref[:, cols]
        for h, vals in zip((2 * tile, 2 * tile + 1), pair(val_ref, tile)):
            gaps = jnp.minimum(logs[:, h : h + 1] - logs_t[h : h + 1], 0.0)
            decay = jnp.exp(gaps) * dt_t[h : h + 1]
            dec_ref[h] = decay.astype(BF16)
            mix = (scores * decay).astype(BF16)
            mix_ref[h] = mix
            total = total + dot(mix, vals, 1, 0)
        inner_ref[:, cols] = total

    mixed = inner_ref[...] + to_units(hp_ref[2:10], lanes)[0:1] * val_ref[...].astype(F32)
    mixed_ref[...] = mixed
    gate = gate_ref[...]
    sig = jax.nn.sigmoid(gate)
    gated = mixed * (gate * sig)
    inverse = lax.rsqrt(jnp.sum(gated * gated, axis=1, keepdims=True) / INNER + EPSILON)
    out_gain = prm_ref[5:6]
    nout_ref[...] = (gated * inverse * out_gain).astype(BF16)
    cot = cot_ref[...]
    branch = x_ref[...].astype(F32)
    for t in range(PARTS):
        cols = slice(t * WIDE, (t + 1) * WIDE)
        w_out = w_ref[t, :, 2 * WIDE : 3 * WIDE]
        branch = branch + dot(nout_ref[:, cols], w_out, 1, 1)
        dout_ref[:, cols] = dot(cot, w_out, 1, 0)
    result_ref[...] = branch.astype(BF16)

    d_out = dout_ref[...]
    normal = gated * inverse
    rows_ref[0:1] = jnp.sum(d_out * normal, axis=0, keepdims=True)
    d_scaled = d_out * out_gain
    dot_total = jnp.sum(d_scaled * normal, axis=1, keepdims=True)
    d_gated = inverse * (d_scaled - normal * (dot_total / INNER))
    d_mixed = d_gated * (gate * sig)
    dgate_ref[...] = (d_gated * mixed * sig * (1.0 + gate * (1.0 - sig))).astype(BF16)
    vals = val_ref[...].astype(F32)
    rows_ref[1:2] = jnp.sum(d_mixed * vals, axis=0, keepdims=True)
    dy_ref[...] = d_mixed.astype(BF16)
    dval_ref[...] = to_units(hp_ref[2:10], lanes)[0:1] * d_mixed

    d_scores = jnp.zeros((ROWS, ROWS), F32)
    dlog = jnp.zeros((ROWS, 128), F32)
    direct = jnp.zeros((ROWS, 128), F32)
    for tile in range(HEADS // 2):
        cols = slice(tile * 128, tile * 128 + 128)
        total = jnp.zeros((ROWS, 128), F32)
        for h, vals, grads in zip((2 * tile, 2 * tile + 1), pair(val_ref, tile), pair(dy_ref, tile)):
            d_mix = dot(grads, vals, 1, 1)
            d_scores = d_scores + d_mix * dec_ref[h].astype(F32)
            total = total + dot(mix_ref[h], grads, 0, 0)
        dval_ref[:, cols] = dval_ref[:, cols] + total
        from_values = total * val_ref[:, cols].astype(F32)
        dout_ref[:, cols] = from_values
    from_values = dout_ref[...]
    direct_ref[...] = to_heads(from_values, lanes)
    dlog_ref[...] = to_heads(dy_ref[...].astype(F32) * inner_ref[...] - from_values, lanes)
    d_scores = jnp.where(allowed, d_scores, 0.0).astype(BF16)
    d_carried = (dy_ref[...].astype(F32) * carried).astype(BF16)
    dscore_ref[:, :STATE] = dot(d_scores, cmat, 0, 0)
    dscore_ref[:, STATE:] = dot(d_scores, bmat, 1, 0) + dot(d_carried, state, 1, 1)
    dstate_ref[...] = dot(cmat, d_carried, 0, 0).astype(BF16)


def leave_kernel(
    val_ref, bc_ref, raw_ref, dt_ref, logs_ref, state_ref, coming_ref, ends_ref, hp_ref,
    dval_ref, dscore_ref, dlog_ref, direct_ref, vpre_ref, vsum_ref, spre_ref, ssum_ref, same_ref,
    dsum_ref, dssum_ref, dstep_ref, heads_ref, rows_ref, srows_ref,
):
    lanes = head_lanes()
    ends = ends_ref[...]
    logs, dt, raw = logs_ref[...], dt_ref[...], raw_ref[...]
    bmat = bc_ref[:, :STATE]
    coming = coming_ref[...]
    last = logs[ROWS - 1 :]
    weights = to_units(ends[:, 0:1] * jnp.exp(last - logs) * dt, lanes)
    vals = val_ref[...].astype(F32)
    weighted = vals * weights
    below = dot(bmat, coming, 1, 0)
    d_values = dval_ref[...] + weights * below
    through = to_heads(weighted * below, lanes)
    d_bees = dscore_ref[:, :STATE] + dot(weighted.astype(BF16), coming, 1, 1)
    kept = ends[0:8, 2:3] * jnp.exp(jnp.broadcast_to(last, (8, 128)))
    held = jnp.sum(coming.astype(F32) * state_ref[...].astype(F32), axis=0, keepdims=True)
    d_kept = to_heads(jnp.broadcast_to(held, (8, INNER)), lanes)
    d_last = jnp.sum(through, axis=0, keepdims=True) + (d_kept * kept)[0:1]
    upper = (lax.broadcasted_iota(jnp.int32, (ROWS, ROWS), 0) <= lax.broadcasted_iota(jnp.int32, (ROWS, ROWS), 1))
    d_rate = dot(upper.astype(F32), dlog_ref[...] - through, 1, 0, HIGHEST) + d_last
    by_rate = dt * hp_ref[1:2] * d_rate
    slope = jnp.where(raw < -15.0, 1.0, jax.nn.sigmoid(raw) / jnp.where(raw < -15.0, 1.0, dt))
    is_head = lax.broadcasted_iota(jnp.int32, (ROWS, 128), 1) < HEADS
    d_step = jnp.where(is_head, (direct_ref[...] + through + by_rate) * slope, 0.0)
    dstep_ref[...] = d_step.astype(BF16)
    heads_ref[...] = jnp.zeros_like(heads_ref)
    heads_ref[0:1] = jnp.sum(d_step, axis=0, keepdims=True)
    heads_ref[1:2] = jnp.sum(by_rate, axis=0, keepdims=True)
    same = same_ref[...]

    def conv_grads(d_sum, before_ref, out_ref):
        out_ref[3:4] = jnp.sum(d_sum * before_ref[HALO:], axis=0, keepdims=True)
        out_ref[4:5] = jnp.sum(d_sum, axis=0, keepdims=True)
        for back in (1, 2, 3):
            shifted = same[:, back : back + 1] * before_ref[HALO - back : HALO - back + ROWS]
            out_ref[3 - back : 4 - back] = jnp.sum(d_sum * shifted, axis=0, keepdims=True)

    d_sum = d_values * silu_slope(vsum_ref[...])
    dsum_ref[...] = d_sum
    rows_ref[...] = jnp.zeros_like(rows_ref)
    conv_grads(d_sum, vpre_ref, rows_ref)
    d_sum = jnp.concatenate([d_bees, dscore_ref[:, STATE:]], axis=1) * silu_slope(ssum_ref[...])
    dssum_ref[...] = d_sum
    srows_ref[...] = jnp.zeros_like(srows_ref)
    conv_grads(d_sum, spre_ref, srows_ref)


def close_kernel(
    x_ref, cot_ref, gain_ref, normed_ref, nout_ref, w_ref, wsh_ref, prm_ref, csh_ref,
    dgate_ref, dsum_ref, dssum_ref, next_ref, snext_ref, dstep_ref, after_ref,
    resid_ref, parts_ref, rows_ref, dval_ref,
):
    after = after_ref[...]

    def conv_back(d_sum, following, taps):
        joined = jnp.concatenate([d_sum, following], axis=0)
        total = taps[3:4] * d_sum
        for ahead in (1, 2, 3):
            total = total + taps[3 - ahead : 4 - ahead] * (after[:, ahead : ahead + 1] * joined[ahead : ahead + ROWS])
        return total.astype(BF16)

    dval_ref[...] = conv_back(dsum_ref[...], next_ref[...], prm_ref[0:4])
    d_shared = conv_back(dssum_ref[...], snext_ref[...], csh_ref[...])
    normed_t = normed_ref[...].T
    cot = cot_ref[...]
    cot_t = cot.T
    dstep = dstep_ref[...]
    step_part = dot(normed_t, dstep, 1, 0)[:, :32].astype(BF16)
    shared_part = dot(normed_t, d_shared, 1, 0).astype(BF16)
    d_normed = dot(pltpu.roll(dstep.astype(F32), 64, 1).astype(BF16), step_weights(w_ref), 1, 1)
    d_normed = d_normed + dot(d_shared, wsh_ref[...], 1, 1)
    for t in range(PARTS):
        cols = slice(t * WIDE, (t + 1) * WIDE)
        both = jnp.concatenate([dgate_ref[:, cols], dval_ref[:, cols]], axis=1)
        parts_ref[t, :, : 2 * WIDE] = dot(normed_t, both, 1, 0).astype(BF16)
        outs = dot(cot_t, nout_ref[:, cols], 1, 0).astype(BF16)
        parts_ref[t, :, 2 * WIDE :] = jnp.concatenate([outs, step_part, shared_part[:, t * 32 : t * 32 + 32]], axis=1)
        d_normed = d_normed + dot(both, w_ref[t, :, : 2 * WIDE], 1, 1)
    x = x_ref[...].astype(F32)
    inverse = lax.rsqrt(jnp.mean(x * x, axis=1, keepdims=True) + EPSILON)
    scaled = x * inverse
    d_in = d_normed * gain_ref[...]
    rows_ref[...] = jnp.sum(d_normed * scaled, axis=0, keepdims=True)
    centred = jnp.mean(d_in * scaled, axis=1, keepdims=True)
    resid_ref[...] = inverse * (d_in - scaled * centred) + cot.astype(F32)


def call(kernel, outs, args, scratch=()):
    return pl.pallas_call(
        kernel,
        out_shape=tuple(jax.ShapeDtypeStruct(shape, dtype) for shape, dtype in outs),
        in_specs=[pl.BlockSpec(memory_space=pltpu.VMEM)] * len(args),
        out_specs=tuple(pl.BlockSpec(memory_space=pltpu.VMEM) for _ in outs),
        scratch_shapes=list(scratch),
        compiler_params=pltpu.CompilerParams(vmem_limit_bytes=VMEM_LIMIT),
    )(*args)


def by_heads(blocks):
    rows = blocks.shape[0]
    pieces = blocks.reshape(rows, PARTS, WIDE).transpose(1, 0, 2)
    return lax.all_to_all(pieces, "tensor", split_axis=0, concat_axis=0, tiled=True)


def by_blocks(pieces):
    back = lax.all_to_all(pieces, "tensor", split_axis=0, concat_axis=0, tiled=True)
    return back.transpose(1, 0, 2).reshape(pieces.shape[1], INNER)


def shards(
    resid_in, cotangent, segments, in_gain, w_gate, w_value, w_step, w_shared, conv_inner, bias_inner,
    conv_shared, bias_shared, step_bias, decay_log, skip_gain, out_gain, w_out,
):
    tensor = lax.axis_index("tensor")
    heads_local = w_step.shape[1]

    extra = lax.dynamic_update_slice(
        jnp.zeros((w_step.shape[0], PACK - 3 * WIDE), BF16), w_step, (jnp.int32(0), tensor * heads_local)
    )
    weights = gather_weights(jnp.concatenate([w_gate, w_value, w_out, extra], axis=1))
    per_head = jnp.stack([step_bias, decay_log, skip_gain])
    own_prm = jnp.concatenate([conv_inner, bias_inner[None], out_gain[None]], axis=0)
    own_prm = jnp.concatenate(
        [own_prm, jnp.pad(per_head.reshape(1, -1), ((0, 0), (0, WIDE - 9))), jnp.zeros((1, WIDE), F32)], axis=0
    )
    all_prm = lax.all_gather(own_prm, "tensor", axis=0)
    prm = all_prm.transpose(1, 0, 2).reshape(8, INNER)
    heads = all_prm[:, 6, :9].reshape(PARTS, 3, heads_local).transpose(1, 0, 2).reshape(3, HEADS)
    heads = jnp.stack([heads[0], -jnp.exp(heads[1]), heads[2]])
    hp = jnp.pad(heads, ((0, 13), (0, 128 - HEADS)))

    ring = [(i, (i + 1) % PARTS) for i in range(PARTS)]
    ahead = lax.ppermute(resid_in[ROWS - HALO :], "tensor", ring)
    tokens = jnp.concatenate([ahead, resid_in], axis=0)
    padded = jnp.concatenate([jnp.full((8,), -1, jnp.int32), segments, jnp.full((8,), -1, jnp.int32)])
    around = lax.dynamic_slice(padded, (tensor * ROWS,), (ROWS + 16,))
    ids = around[8 : 8 + ROWS]
    lanes8 = lambda columns: jnp.stack(columns + [jnp.zeros((ROWS,), F32)] * (8 - len(columns)), axis=1)
    same = lanes8([jnp.ones((ROWS,), F32)] + [(around[8 - k : 8 - k + ROWS] == ids).astype(F32) for k in (1, 2, 3)])
    after = lanes8([jnp.ones((ROWS,), F32)] + [(around[8 + k : 8 + k + ROWS] == ids).astype(F32) for k in (1, 2, 3)])
    before, last = around[7], ids[ROWS - 1]
    ends = lanes8([
        (ids == last).astype(F32), (ids == before).astype(F32),
        jnp.broadcast_to((last == before).astype(F32), (ROWS,)), ids.astype(F32),
    ])
    ids_row = ids.astype(F32)[None]

    big, small, heads_f = (ROWS, INNER), (ROWS, 2 * STATE), (ROWS, 128)
    normed, gate, vpre, vsum, vals, spre, ssum, bc, raw, dt, logs, fresh = call(
        enter_kernel,
        [
            ((ROWS, D), BF16), (big, F32), ((ROWS + HALO, INNER), F32), (big, F32), (big, BF16),
            ((ROWS + HALO, 2 * STATE), F32), (small, F32), (small, BF16),
            (heads_f, F32), (heads_f, F32), (heads_f, F32), ((STATE + 16, INNER), BF16),
        ],
        (tokens, in_gain[None], weights, w_shared, prm, hp, conv_shared, bias_shared[None], same, ends),
    )

    arrived = by_heads(fresh).astype(F32)
    kept = arrived[:, STATE] + arrived[:, STATE + 1]
    state, states = jnp.zeros((STATE, WIDE), F32), []
    for block in range(PARTS):
        states.append(state.astype(BF16))
        state = arrived[block, :STATE] + kept[block][None] * state
    state = by_blocks(jnp.stack(states))

    result, nout, dgate, dval, dscore, dstate, dlog, direct, rows_out = call(
        middle_kernel,
        [
            ((ROWS, D), BF16), (big, BF16), (big, BF16), (big, F32), (small, F32), ((STATE, INNER), BF16),
            (heads_f, F32), (heads_f, F32), ((8, INNER), F32),
        ],
        (resid_in, cotangent, weights, prm, hp, gate, vals, bc, dt, logs, state, ends, ids_row),
        [
            pltpu.VMEM((HEADS, ROWS, ROWS), BF16), pltpu.VMEM((HEADS, ROWS, ROWS), BF16),
            pltpu.VMEM(big, F32), pltpu.VMEM(big, F32), pltpu.VMEM(big, F32), pltpu.VMEM(big, BF16),
        ],
    )

    arrived = by_heads(dstate).astype(F32)
    coming, comings = jnp.zeros((STATE, WIDE), F32), [None] * PARTS
    for block in reversed(range(PARTS)):
        comings[block] = coming.astype(BF16)
        coming = arrived[block] + kept[block][None] * coming
    coming = by_blocks(jnp.stack(comings))

    dsum, dssum, dstep, head_rows, rows_conv, srows_conv = call(
        leave_kernel,
        [
            (big, F32), (small, F32), (heads_f, BF16), ((8, 128), F32), ((8, INNER), F32), ((8, 2 * STATE), F32),
        ],
        (
            vals, bc, raw, dt, logs, state, coming, ends, hp, dval, dscore, dlog, direct,
            vpre, vsum, spre, ssum, same,
        ),
    )
    back_ring = [(i, (i - 1) % PARTS) for i in range(PARTS)]
    following = lax.ppermute(jnp.concatenate([dsum[:8], dssum[:8]], axis=1), "tensor", back_ring)
    grad_resid, parts, rows_in = call(
        close_kernel,
        [((ROWS, D), F32), ((PARTS, D, PACK), BF16), ((1, D), F32)],
        (
            resid_in, cotangent, in_gain[None], normed, nout, weights, w_shared, prm, conv_shared, dgate,
            dsum, dssum, following[:, :INNER], following[:, INNER:], dstep, after,
        ),
        [pltpu.VMEM(big, BF16)],
    )

    pieces = [
        rows_conv[:5], rows_out[:2], srows_conv[:5], head_rows[:2], rows_in,
    ]
    flat = jnp.concatenate([piece.reshape(-1) for piece in pieces])
    rows = -(-flat.size // 1024) * 8
    flat = jnp.pad(flat, (0, rows * 128 - flat.size)).reshape(rows, 128)
    block, tails, flat = reduce_grads(parts, flat)
    flat = flat.reshape(-1)
    sums, at = [], 0
    for piece in pieces:
        sums.append(flat[at : at + piece.size].reshape(piece.shape))
        at += piece.size
    inner_rows, out_rows, shared_rows, head_sums, gain_row = sums
    mine = lambda row: lax.dynamic_slice_in_dim(row, tensor * WIDE, WIDE, axis=-1)
    own_heads = lambda row: lax.dynamic_slice_in_dim(row, tensor * heads_local, heads_local, axis=-1)
    grad_w_shared = tails[:, :, TAIL - 32 :].transpose(1, 0, 2).reshape(D, 2 * STATE).astype(F32)
    return (
        result,
        grad_resid,
        gain_row[0],
        block[:, :WIDE],
        block[:, WIDE : 2 * WIDE],
        own_heads(block[:, 3 * WIDE : 3 * WIDE + HEADS]),
        grad_w_shared,
        mine(inner_rows[:4]),
        mine(inner_rows[4]),
        shared_rows[:4],
        shared_rows[4],
        own_heads(head_sums[0]),
        own_heads(head_sums[1]),
        mine(out_rows[1]).reshape(heads_local, HEADDIM).sum(axis=1),
        mine(out_rows[0]),
        block[:, 2 * WIDE : 3 * WIDE],
    )


def solution(mesh):
    rows, cols = P(("dp", "tensor"), None), P("dp", "tensor")
    head, whole = P("tensor"), P()
    in_specs = (
        rows, rows, P("dp"), whole, cols, cols, cols, whole, P(None, "tensor"), head,
        whole, whole, head, head, head, head, cols,
    )
    out_specs = (
        rows, rows, whole, cols, cols, cols, whole, P(None, "tensor"), head,
        whole, whole, head, head, head, head, cols,
    )
    return jax.shard_map(shards, mesh=mesh, in_specs=in_specs, out_specs=out_specs, check_vma=False)
```

time: 864 us -> 278 us (0.32); the launches traced: 853 us -> 277 us
  local copies, waits for them, and re-layouts: 225 us -> 37.4 us
  matrix products: 172 us -> 0 us
  Pallas kernels: 0 us -> 154 us
  other arithmetic: 131 us -> 13.1 us
  blocking collectives: 153 us -> 43.8 us
  waiting for transfers between devices: 100 us -> 14.5 us
  starting transfers between devices: 34.9 us -> 11.1 us
  loops' own time: 22.6 us -> 0 us
  between operations: 15.6 us -> 2.21 us
    dot_general x111 -> x0, matrix products: 159 us -> none  [the longest x24 46.9 us: advance(): inside = jnp.einsum('hts,shp->thp', mixing, vals, precision=HIGHEST)]
    pallas_call x0 -> x6, Pallas kernels: none -> 154 us  [the longest x1 61.6 us: reduce_grads(): pl.pallas_call(body, out_shape=(jax.ShapeDtypeStruct((3, 16, PACK), F32),...]
    dynamic_update_slice x48 -> x1, local copies, waits for them, and re-layouts: 106 us -> 0.16 us  [shards(): lax.dynamic_update_slice(jnp.zeros((w_step.shape[0], PACK - 3 * WIDE), BF...]
    psum x1 -> x0, waiting for transfers between devices: 74.2 us -> none  [shards(): lax.psum((shared_weight_part, in_gain_part, g_conv_shared, g_bias_shared)...]
    psum x1 -> x0, blocking collectives: 71.9 us -> none  [shards(): lax.psum((shared_weight_part, in_gain_part, g_conv_shared, g_bias_shared)...]
    all_gather x2 -> x1, blocking collectives: 72.3 us -> 22.1 us  [shards(): all_prm = lax.all_gather(own_prm, 'tensor', axis=0)]
    another operation x57 -> x4, other arithmetic: 45.7 us -> 2.79 us  [the longest x1 1.38 us: shards(): jnp.stack(columns + [jnp.zeros((ROWS,), F32)] * (8 - len(columns)), axis=1)]
    all_to_all x7 -> x2, starting transfers between devices: 34.3 us -> 7.21 us  [the longest x1 3.67 us: by_blocks(): lax.all_to_all(pieces, 'tensor', split_axis=0, concat_axis=0, tiled=True)]
  transfers between devices with their start and end apart: 13 -> 4, of which waited for: 7 -> 3; matrix products, arithmetic and copies ran while one was open for 61% -> 5% of each run, Pallas kernels for 0% -> 16%
where the time goes in v1:
time: 278 us; the launch traced here: 277 us
  Pallas kernels  154 us (55%)
  blocking collectives  43.8 us (16%)
  local copies, waits for them, and re-layouts  37.4 us (13%)
  waiting for transfers between devices  14.5 us (5%)
  other arithmetic  13.1 us (5%)
  starting transfers between devices  11.1 us (4%)
    pallas_call x1, Pallas kernels, reduce_grads(): pl.pallas_call(body, out_shape=(jax.ShapeDtypeStruct((3, 16, PACK), F32),...  61.6 us
    pallas_call x4, Pallas kernels, call(): pl.pallas_call(kernel, out_shape=tuple((jax.ShapeDtypeStruct(shape, dtype...  47.5 us
    pallas_call x1, Pallas kernels, gather_weights(): pl.pallas_call(gather_kernel, out_shape=jax.ShapeDtypeStruct((2, 4, 4, 2,...  45.3 us
    all_gather x1, blocking collectives, shards(): all_prm = lax.all_gather(own_prm, 'tensor', axis=0)  22.1 us
    all_to_all x1, blocking collectives, by_blocks(): lax.all_to_all(pieces, 'tensor', split_axis=0, concat_axis=0, tiled=True)  11.8 us
    all_to_all x1, blocking collectives, by_heads(): lax.all_to_all(pieces, 'tensor', split_axis=0, concat_axis=0, tiled=True)  9.85 us
    all_to_all x1, waiting for transfers between devices, by_heads(): lax.all_to_all(pieces, 'tensor', split_axis=0, concat_axis=0, tiled=True)  9.27 us
    unnamed x14, other arithmetic  5.72 us
  transfers between devices with their start and end apart: 4, of which 3 were waited for; matrix products, arithmetic and copies ran while one was open for 5% of the time, Pallas kernels for 16%

profile of v1, /device:TPU:1, one launch (start us, length us, event | category | flops | bytes accessed | tf_op | source)
XLA Modules:
  0.0 276.6 jit_solution(16935700007825959738)
XLA Ops:
  0.6 0.7 slice.238
  1.4 2.1 collective-permute-start
  3.5 0.8 concatenate.21
  5.8 0.8 copy.108
  6.6 0.7 concatenate.19
  7.3 22.1 %all-gather = f32[64,192]{1,0:T(8,128)S(1)} all-gather(f32[8,192]{1,0:T(8,128)S(1)} %concatenate.19), channel_id=2, replica_groups=mesh['dp'=16,'tensor'=8] {'tensor'}, dimensions={0}, use_global_device_ids=true | all-gather | bytes 55296 | tf_op jit(solution)/shard_map/all_gather | solution.py:650
  30.1 1.4 compare_convert_fusion
  31.6 1.5 pad_maximum_fusion.1
  35.0 1.3 broadcast_in_dim.26.gain_ref
  37.0 0.8 copy.115.ends_ref
  37.9 0.8 copy.114.same_ref
  38.7 45.3 %shard_map.288 = bf16[2,4,4,2,2,3,16,640]{7,6,5,4,3,2,1,0:T(8,128)(2,1)} custom-call(bf16[3,16,640]{2,1,0:T(8,128)(2,1)} %bitcast.77), custom_call_target="tpu_custom_call" | custom-call | tf_op jit(solution)/shard_map/pallas_call | solution.py:139
  84.0 0.8 pad_maximum_fusion.x_ref
  84.8 11.4 %shard_map.289 = (bf16[256,768]{1,0:T(8,128)(2,1)}, f32[256,1536]{1,0:T(8,128)}, f32[272,1536]{1,0:T(8,128)}, f32[256,1536]{1,0:T(8,128)}, bf16[256,1536]{1,0:T(...) custom-call(bf16[272,768]{1,0:T(8,128)(2,1)} %pad_maximum_fusion.x_r, ...), custom_call_target="tpu_custom_call" | custom-call | tf_op jit(solution)/shard_map/pallas_call | solution.py:613
  96.3 1.5 reshape.488
  97.8 0.9 copy.133
  98.7 3.5 %all-to-all-start = ((bf16[8,144,192]{2,1,0:T(8,128)(2,1)}), bf16[8,144,192]{2,1,0:T(8,128)(2,1)S(1)}, u32[]{:S(2)}, u32[]{:S(2)}) async-start(bf16[8,144,192]{2,1,0:T(8,128)(2,1)} %bitcast.61), calls=%async_computation | async-start | bytes 1179648 | tf_op jit(solution)/shard_map/all_to_all | solution.py:626
  102.3 9.3 %all-to-all-done = bf16[8,144,192]{2,1,0:T(8,128)(2,1)S(1)} async-done(((bf16[8,144,192]{2,1,0:T(8,128)(2,1)}), bf16[8,144,192]{2,1,0:T(8,128)(2,1)S(1)}, u32[]{:S(2)}, u32[]{:S(2)}) %all-to-all-start) | async-done | bytes 442400 | tf_op jit(solution)/shard_map/all_to_all | solution.py:626
  113.5 11.8 %all_to_all.20 = bf16[8,128,192]{1,2,0:T(8,128)(2,1)S(1)} all-to-all(bf16[8,128,192]{1,2,0:T(8,128)(2,1)S(1)} %fusion.8), channel_id=1, replica_groups=mesh['dp'=16,'tensor'=8] {'tensor'}, dimensions={0} | all-to-all | bytes 786432 | tf_op jit(solution)/shard_map/all_to_all | solution.py:630
  125.4 0.9 copy.118.state_ref
  126.3 14.3 %shard_map.290 = (bf16[256,768]{1,0:T(8,128)(2,1)}, bf16[256,1536]{1,0:T(8,128)(2,1)}, bf16[256,1536]{1,0:T(8,128)(2,1)}, f32[256,1536]{1,0:T(8,128)}, f32[256,2...) custom-call(bf16[256,768]{1,0:T(8,128)(2,1)} %x_ref.3, ...), custom_call_target="tpu_custom_call" | custom-call | tf_op jit(solution)/shard_map/pallas_call | solution.py:613
  140.6 1.2 copy.120
  141.8 9.9 %all_to_all.21 = bf16[8,128,192]{1,2,0:T(8,128)(2,1)S(1)} all-to-all(bf16[8,128,192]{1,2,0:T(8,128)(2,1)S(1)} %bitcast.73), channel_id=1, replica_groups=mesh['dp'=16,'tensor'=8] {'tensor'}, dimensions={0} | all-to-all | bytes 786432 | tf_op jit(solution)/shard_map/all_to_all | solution.py:626
  151.7 0.9 fusion.9
  152.6 0.7 convert_dynamic-update-slice_fusion.4
  154.0 0.7 convert_dynamic-update-slice_fusion.2
  155.3 0.7 convert_dynamic-update-slice_fusion
  156.0 0.7 fusion.6
  157.4 3.7 %all-to-all-start.3 = ((bf16[8,128,192]{1,2,0:T(8,128)(2,1)}), bf16[8,128,192]{1,2,0:T(8,128)(2,1)S(1)}, u32[]{:S(2)}, u32[]{:S(2)}) async-start(bf16[8,128,192]{1,2,0:T(8,128)(2,1)} %constant_dynamic-update-slice_fusion.1), calls=%async_computation.3 | async-start | bytes 786432 | tf_op jit(solution)/shard_map/all_to_all | solution.py:630
  161.1 0.8 copy.125.after_ref
  161.9 0.8 slice.277
  162.7 4.7 %all-to-all-done.3 = bf16[8,128,192]{1,2,0:T(8,128)(2,1)S(1)} async-done(((bf16[8,128,192]{1,2,0:T(8,128)(2,1)}), bf16[8,128,192]{1,2,0:T(8,128)(2,1)S(1)}, u32[]{:S(2)}, u32[]{:S(2)}) %all-to-all-start.3) | async-done | bytes 393248 | tf_op jit(solution)/shard_map/all_to_all | solution.py:630
  167.4 0.9 copy.122.coming_ref
  168.3 7.8 %shard_map.291 = (f32[256,1536]{1,0:T(8,128)}, f32[256,256]{1,0:T(8,128)}, bf16[256,128]{1,0:T(8,128)(2,1)}, f32[8,128]{1,0:T(8,128)}, f32[8,1536]{1,0:T(8,128)}, /*index=5*/f32[8,256]{1,0:T(8,128)}) custom-call(bf16[256,1536]{1,0:T(8,128)(2,1)} %get-tuple-element.50.val_ref, bf16[256,256]{1,0:T(8,128)(2,1)} %get-tuple-element.51.bc_ref, ...), custom_call_target="tpu_custom_call" | custom-call | tf_op jit(solution)/shard_map/pallas_call | solution.py:613
  176.2 0.8 reshape.493
  178.4 0.8 slice.269
  179.2 1.8 collective-permute-start.1
  183.5 13.8 %shard_map.292 = (f32[256,768]{1,0:T(8,128)}, bf16[8,768,640]{2,1,0:T(8,128)(2,1)}, f32[1,768]{1,0:T(1,128)}) custom-call(bf16[256,768]{1,0:T(8,128)(2,1)} %x_ref.3, bf16[256,768]{1,0:T(8,128)(2,1)} %cot_ref.3, f32[1,768]{1,0:T(1,128)} %broadcast_in_dim.26.gain_ref, bf16[256,768]{1,0:T(8,128)(2,1)} %get-tuple-element.56.normed_ref, ...), custom_call_target="tpu_custom_call" | custom-call | tf_op jit(solution)/shard_map/pallas_call | solution.py:613
  198.7 61.6 %shard_map.293 = (f32[3,16,640]{2,1,0:T(8,128)}, bf16[2,4,4,2,2,3,16,128]{7,6,5,4,3,2,1,0:T(8,128)(2,1)}, f32[104,128]{1,0:T(8,128)}) custom-call(bf16[2,4,4,2,2,3,16,640]{7,6,5,4,3,2,1,0:T(8,128)(2,1)} %bitcast.68, f32[104,128]{1,0:T(8,128)} %pad_bitcast_fusion.small_ref), custom_call_target="tpu_custom_call" | custom-call | tf_op jit(solution)/shard_map/pallas_call | solution.py:307
  260.3 1.2 slice_bitcast_fusion.4
  261.5 0.7 fusion.14
  263.0 1.3 slice_bitcast_fusion.3
  264.2 0.7 slice.286
  265.0 0.8 slice_bitcast_fusion
  265.7 0.8 slice.329
  266.6 1.6 fusion.13
  268.2 1.9 slice.330
  274.8 1.1 copy.128
  (79 shorter events, 18.9 us)
Async XLA Ops:
  1.4 82.6 %collective-permute-start = (bf16[16,768]{1,0:T(8,128)(2,1)S(1)}, bf16[16,768]{1,0:T(8,128)(2,1)S(1)}, u32[]{:S(2)}, u32[]{:S(2)}) collective-permute-start(bf16[16,768]{1,0:T(8,128)(2,1)S(1)} %slice.238), channel_id=1, source_target_pairs={{0,1},{1,2},{2,3},{3,4},{4,5},{5,6},{6,7},{7,0},{8,9},{9,10},{10,1... | collective-permute-start | bytes 73736 | tf_op jit(solution)/shard_map/ppermute | solution.py:657
  4.4 79.6 %copy-start.1 = (f32[256]{0:T(256)}, f32[256]{0:T(256)S(1)}, u32[]{:S(2)}) copy-start(f32[256]{0:T(256)S(1)} %slice_convert_fusion) | copy-start | bytes 3076
  38.7 45.4 %copy-start = (bf16[256,768]{1,0:T(8,128)(2,1)S(1)}, bf16[256,768]{1,0:T(8,128)(2,1)}, u32[]{:S(2)}) copy-start(bf16[256,768]{1,0:T(8,128)(2,1)} %x_ref.3) | copy-start | bytes 1179652
  98.7 12.8 %all-to-all-start = ((bf16[8,144,192]{2,1,0:T(8,128)(2,1)}), bf16[8,144,192]{2,1,0:T(8,128)(2,1)S(1)}, u32[]{:S(2)}, u32[]{:S(2)}) async-start(bf16[8,144,192]{2,1,0:T(8,128)(2,1)} %bitcast.61), calls=%async_computation | async-start | bytes 1179648 | tf_op jit(solution)/shard_map/all_to_all | solution.py:626
  157.4 10.0 %all-to-all-start.3 = ((bf16[8,128,192]{1,2,0:T(8,128)(2,1)}), bf16[8,128,192]{1,2,0:T(8,128)(2,1)S(1)}, u32[]{:S(2)}, u32[]{:S(2)}) async-start(bf16[8,128,192]{1,2,0:T(8,128)(2,1)} %constant_dynamic-update-slice_fusion.1), calls=%async_computation.3 | async-start | bytes 786432 | tf_op jit(solution)/shard_map/all_to_all | solution.py:630
  179.2 3.1 %collective-permute-start.1 = (f32[8,1792]{1,0:T(8,128)S(1)}, f32[8,1792]{1,0:T(8,128)S(1)}, u32[]{:S(2)}, u32[]{:S(2)}) collective-permute-start(f32[8,1792]{1,0:T(8,128)S(1)} %pad_maximum_fusion.2), channel_id=1, source_target_pairs={{0,7},{1,0},{2,1},{3,2},{4,3},{5,4},{6,5},{7,6},{8,15},{9,8},{10,9... | collective-permute-start | bytes 172040 | tf_op jit(solution)/shard_map/ppermute | solution.py:722

commit v2 on v0

v2 whole, which is shorter than its diff:
```python
import types

import jax
import jax.numpy as jnp
from jax import lax
from jax.experimental import pallas as pl
from jax.experimental.pallas import tpu as pltpu
from jax.sharding import PartitionSpec as P

D = 768
HEADS = 24
HEADDIM = 64
STATE = 128
INNER = 1536
ROWS = 256
HALO = 16
PARTS = 8
WIDE = 192
PACK_V = 256
PACK_G = 384
EPSILON = 1e-05
VMEM_LIMIT = 62 * 1024 * 1024
MESH = pl.DeviceIdType.MESH
HIGHEST = lax.Precision.HIGHEST
F32 = jnp.float32
BF16 = jnp.bfloat16

ORDERS = (("x", "y", "z"), ("y", "z", "x"), ("z", "x", "y"))
DIMS = ("x", "y", "z")
ASIDE = (("x", "y", "z"), ("y", "x", "z"), ("z", "y", "x"))
EVERY = slice(None)


def place():
    dp, tensor = lax.axis_index("dp"), lax.axis_index("tensor")
    x = (dp // 2 % 2) * 2 + tensor // 4
    return {"x": x, "y": tensor % 4, "z": dp // 4, "core": dp % 2, "dp": dp, "t": tensor}


def device_of(at):
    return (at["z"] * 4 + (at["x"] // 2) * 2 + at["core"], (at["x"] % 2) * 4 + at["y"])


def moved(me, dim, by):
    return {**me, dim: (me[dim] + by) % 4}


def sibling(me):
    return {**me, "core": 1 - me["core"]}


def region(fixed, half=None):
    x_lo, x_hi = (fixed["x"] % 2, fixed["x"] // 2) if "x" in fixed else (EVERY, EVERY)
    y, z = fixed.get("y", EVERY), fixed.get("z", EVERY)
    if half is not None:
        if "x" not in fixed:
            x_lo = pl.ds(half, 1)
        else:
            y = pl.ds(half * 2, 2)
    return (x_lo, y, z, x_hi)


def free_shape(fixed, half=False):
    sizes = [[dim, size] for dim, size in (("x", 2), ("y", 4), ("z", 4), ("x", 2)) if dim not in fixed]
    if half:
        sizes[0][1] //= 2
    return tuple(size for dim, size in sizes)


def transfer(src, dst, sems, slot, target):
    copy = pltpu.make_async_remote_copy(
        src_ref=src,
        dst_ref=dst,
        send_sem=sems[0].at[slot],
        recv_sem=sems[1].at[slot],
        device_id=target,
        device_id_type=MESH,
    )
    copy.start()
    return copy


def send(src, dst, sems, slot, target):
    return transfer(src, dst, sems, slot, device_of(target))


def peer(me, step):
    z_x = (me["z"] * 2 + me["x"] // 2 + step // 8) % 8
    return (z_x * 2 + me["core"], (me["t"] + step % 8) % 8)


def each_peer(body):
    def step(i, carry):
        body(i)
        return carry

    lax.fori_loop(1, 64, step, 0)


def neighbours(me):
    along = [device_of(moved(me, dim, by)) for dim in DIMS for by in (1, 2, 3)]
    return along + [device_of(sibling(me))] + [(me["dp"], ((me["t"] + 4) % 8 // 4) * 4 + (me["y"] + by) % 4) for by in (1, 2, 3)]


def greet(me):
    for other in neighbours(me):
        pl.semaphore_signal(pltpu.get_barrier_semaphore(), inc=1, device_id=other, device_id_type=MESH)


def greeted():
    pl.semaphore_wait(pltpu.get_barrier_semaphore(), 13)


GATHER_SLOTS = 15
REDUCE_SLOTS = 14


class Gather:
    def __init__(self, me, own, buf, sems, relayed):
        self.me, self.own, self.buf, self.sems, self.relayed = me, own, buf, sems, relayed
        self.sent, self.got = [], {}

    def unit(self, p, stage, value, half=None):
        order = ORDERS[p]
        fixed = {dim: self.me[dim] for dim in order[stage + 1 :]}
        fixed[order[stage]] = value
        return self.buf.at[region(fixed, half) + (self.me["core"], p)]

    def go(self, name, p, slot, piece, target, source=None):
        copy = send(piece if source is None else source, piece, self.sems, p * GATHER_SLOTS + slot, target)
        self.sent.append(copy)
        self.got[name, p] = copy

    def first(self):
        me = self.me
        for p in range(3):
            dim = ORDERS[p][0]
            for by in (1, 3, 2):
                self.go(("a", by), p, by - 1, self.unit(p, 0, me[dim]), moved(me, dim, by), self.own.at[p])
        here = region({dim: me[dim] for dim in DIMS}) + (me["core"],)
        self.buf[here] = self.own[...]

    def second(self):
        me = self.me
        for p in range(3):
            for by in (1, 3, 2):
                self.got[("a", by), p].wait_recv()
            dim = ORDERS[p][1]
            for by in (1, 3, 2):
                self.go(("b", by), p, 2 + by, self.unit(p, 1, me[dim]), moved(me, dim, by))

    def third(self):
        me = self.me
        for p in range(3):
            for by in (1, 3, 2):
                self.got[("b", by), p].wait_recv()
            dim = ORDERS[p][2]
            unit = self.unit(p, 2, me[dim])
            self.go(("c", 1), p, 6, unit, moved(me, dim, 1))
            self.go(("c", 3), p, 7, unit, moved(me, dim, 3))
            if not self.relayed:
                self.go(("c", 2), p, 8, unit, moved(me, dim, 2))
        for p in range(3):
            self.across(p, 10, me[ORDERS[p][2]])

    def across(self, p, slot, value, half=None):
        self.go(("s", slot), p, slot, self.unit(p, 2, value, half), sibling(self.me))

    def relay(self):
        me = self.me
        for p in range(3):
            dim = ORDERS[p][2]
            for step, by, half in ((1, 1, 0), (3, 3, 1)):
                self.got[("c", by), p].wait_recv()
                value = (me[dim] - by) % 4
                if self.relayed:
                    self.go(("r", half), p, 8 + half, self.unit(p, 2, value, half), moved(me, dim, by))
                self.across(p, 11 + half, value)

    def finish(self):
        me = self.me
        for p in range(3):
            across = (me[ORDERS[p][2]] + 2) % 4
            if self.relayed:
                for half in (0, 1):
                    self.got[("r", half), p].wait_recv()
                    self.across(p, 13 + half, across, half)
            else:
                self.got[("c", 2), p].wait_recv()
                self.across(p, 13, across)

    def settle(self):
        for p in range(3):
            for slot in (10, 11, 12, 13, 14) if self.relayed else (10, 11, 12, 13):
                self.got[("s", slot), p].wait_recv()

    def drain(self):
        for copy in self.sent:
            copy.wait_send()


class Reduce:
    def __init__(self, me, orders, parts, heard, relayed, got_c, got_b, got_a, sems):
        self.me, self.orders, self.parts, self.sems = me, orders, parts, sems
        self.heard, self.relayed, self.got_c, self.got_b, self.got_a = heard, relayed, got_c, got_b, got_a
        self.sent, self.got = [], {}

    def unit(self, p, stage, by, half=None):
        order = self.orders[p]
        fixed = {dim: self.me[dim] for dim in order[stage + 1 :]}
        fixed[order[stage]] = (self.me[order[stage]] + by) % 4
        return region(fixed, half)

    def mine(self, p, stage, by, half=None):
        return self.unit(p, stage, by, half) + (self.me["core"], p)

    def go(self, name, p, slot, src, dst, target):
        copy = send(src, dst, self.sems, p * REDUCE_SLOTS + slot, target)
        self.sent.append(copy)
        self.got[name, p] = copy

    def swap(self):
        me = self.me
        for by in (2, 1, 3, 0):
            for p in range(3):
                src = self.parts.at[self.unit(p, 2, by) + (1 - me["core"], p)]
                self.go(("s", by), p, by, src, self.heard[p].at[by], sibling(me))

    def heard_add(self, by):
        for p in range(3):
            self.got[("s", by), p].wait_recv()
            at = self.mine(p, 2, by)
            self.parts[at] = self.parts[at] + self.heard[p][by]

    def relay(self):
        for by in (2, 1, 3):
            self.heard_add(by)
            for p in range(3):
                dim = self.orders[p][2]
                if self.relayed is None:
                    src, dst = self.parts.at[self.mine(p, 2, by)], self.got_c[p].at[by - 1]
                    self.go(("c", by), p, 3 + by, src, dst, moved(self.me, dim, by))
                elif by == 2:
                    for to, half in ((1, 0), (3, 1)):
                        src = self.parts.at[self.mine(p, 2, 2, half)]
                        self.go(("r", half), p, 4 + half, src, self.relayed[p].at[half], moved(self.me, dim, to))

    def third(self):
        for p in range(3):
            dim = self.orders[p][2]
            for by, half in ((1, 0), (3, 1)):
                if self.relayed is not None:
                    self.got[("r", half), p].wait_recv()
                    at = self.mine(p, 2, by, half)
                    self.parts[at] = self.parts[at] + self.relayed[p][half]
                    src = self.parts.at[self.mine(p, 2, by)]
                    self.go(("c", by), p, 6 + half, src, self.got_c[p].at[half], moved(self.me, dim, by))
        self.heard_add(0)

    def second(self):
        for p in range(3):
            for by in (1, 3) if self.relayed is not None else (1, 3, 2):
                self.got[("c", by), p].wait_recv()
            at, got = self.mine(p, 2, 0), self.got_c[p]
            summed = self.parts[at].astype(F32) + (got[0].astype(F32) + got[1].astype(F32))
            if self.relayed is None:
                summed = summed + got[2].astype(F32)
            self.parts[at] = summed.astype(BF16)
            dim = self.orders[p][1]
            for by in (1, 3, 2):
                self.go(("b", by), p, 7 + by, self.parts.at[self.mine(p, 1, by)], self.got_b[p].at[by - 1], moved(self.me, dim, by))

    def first(self):
        for p in range(3):
            for by in (1, 3, 2):
                self.got[("b", by), p].wait_recv()
            at, got = self.mine(p, 1, 0), self.got_b[p]
            self.parts[at] = (
                (self.parts[at].astype(F32) + got[0].astype(F32)) + (got[1].astype(F32) + got[2].astype(F32))
            ).astype(BF16)
            dim = self.orders[p][0]
            for by in (1, 3, 2):
                self.go(("a", by), p, 10 + by, self.parts.at[self.mine(p, 0, by)], self.got_a.at[p, by - 1], moved(self.me, dim, by))

    def result(self, p):
        for by in (1, 3, 2):
            self.got[("a", by), p].wait_recv()
        got = self.got_a
        return (self.parts[self.mine(p, 0, 0)].astype(F32) + got[p, 0].astype(F32)) + (
            got[p, 1].astype(F32) + got[p, 2].astype(F32)
        )

    def drain(self):
        for copy in self.sent:
            copy.wait_send()


class Total:
    def __init__(self, me, own, sums, got, sems):
        self.me, self.own, self.sums, self.got, self.sems = me, own, sums, got, sems
        self.sent = []

    def along(self, stage):
        me, src = self.me, self.own if stage == 0 else self.sums.at[stage - 1]
        if stage == 0:
            peers = [(9, sibling(me))]
        else:
            dim = DIMS[3 - stage]
            peers = [((stage - 1) * 3 + by - 1, moved(me, dim, by)) for by in (1, 3, 2)]
        self.now = [send(src, self.got.at[slot], self.sems, slot, peer) for slot, peer in peers]
        self.sent += self.now

    def add(self, stage):
        for copy in self.now:
            copy.wait_recv()
        got = self.got
        if stage == 0:
            self.sums[0] = self.own[...] + got[9]
        else:
            base = (stage - 1) * 3
            self.sums[stage] = (self.sums[stage - 1] + got[base]) + (got[base + 1] + got[base + 2])

    def drain(self):
        for copy in self.sent:
            copy.wait_send()


class Shared:
    def __init__(self, me, tiles, heard, got, own, tails, sems):
        self.me, self.tiles, self.heard, self.got, self.own, self.tails = me, tiles, heard, got, own, tails
        self.sems = sems
        self.sent = []

    def at(self, device):
        return (device[0] // 4, device[0] // 2 % 2, device[0] % 2, device[1])

    def here(self):
        return self.at((self.me["dp"], self.me["t"]))

    def half(self, core):
        return (EVERY, EVERY, core)

    def across(self, src, dst, slot):
        copy = send(src, dst, self.sems, slot, sibling(self.me))
        self.sent.append(copy)
        return copy

    def swap(self):
        self.swapped = self.across(self.tiles.at[self.half(1 - self.me["core"])], self.heard, 0)

    def everyone(self, src, dst, slot):
        def go(i):
            to = peer(self.me, i)
            pltpu.make_async_remote_copy(
                src_ref=src(to), dst_ref=dst, send_sem=self.sems[0].at[slot], recv_sem=self.sems[1].at[slot],
                device_id=to, device_id_type=MESH,
            ).start()

        each_peer(go)

    def wait(self, kind, slot):
        all_tiles = self.got.at[pl.ds(0, 63)]
        pltpu.make_async_copy(all_tiles, all_tiles, self.sems[kind].at[slot]).wait()

    def scatter(self):
        self.swapped.wait_recv()
        mine = self.half(self.me["core"])
        self.tiles[mine] = self.tiles[mine] + self.heard[...]
        z, x_hi, _, t = self.here()
        place = (z * 2 + x_hi) * 8 + t
        self.everyone(lambda to: self.tiles.at[self.at(to)], self.got.at[place], 1)
        self.got[place] = self.tiles[self.here()]

    def gather(self):
        self.wait(1, 1)
        total = jnp.sum(self.got[...].astype(F32), axis=0).astype(BF16)
        self.own[...] = total
        self.everyone(lambda to: self.own, self.tails.at[self.here()], 2)
        self.tails[self.here()] = total

    def share(self):
        self.wait(1, 2)
        mine = self.tails.at[self.half(self.me["core"])]
        self.shared = self.across(mine, mine, 3)

    def finish(self):
        self.shared.wait_recv()

    def drain(self):
        self.wait(0, 1)
        self.wait(0, 2)
        for copy in self.sent:
            copy.wait_send()


class Swap:
    def __init__(self, me, src, got, sems):
        self.me, self.src, self.got, self.sems = me, src, got, sems
        self.copies = []

    def start(self):
        dp, t = self.me["dp"], self.me["t"]
        for by in (4, 2, 6, 1, 7, 3, 5):
            to = (t + by) % PARTS
            self.copies.append(transfer(self.src.at[to], self.got.at[t], self.sems, by, (dp, to)))
        self.got[t] = self.src[t]

    def wait(self):
        for copy in self.copies:
            copy.wait_recv()

    def drain(self):
        for copy in self.copies:
            copy.wait_send()


def dot(a, b, over_a, over_b, precision=None):
    return lax.dot_general(
        a, b, (((over_a,), (over_b,)), ((), ())), precision=precision, preferred_element_type=F32
    )


def head_lanes():
    head = lax.broadcasted_iota(jnp.int32, (128, INNER), 0)
    unit = lax.broadcasted_iota(jnp.int32, (128, INNER), 1)
    low = head * HEADDIM
    return jnp.where((unit >= low) & (unit < low + HEADDIM), 1.0, 0.0).astype(BF16)


def halves(v):
    top = v.astype(BF16)
    return top, (v - top.astype(F32)).astype(BF16)


def to_units(v, lanes):
    top, rest = halves(v)
    return dot(top, lanes, 1, 0) + dot(rest, lanes, 1, 0)


def to_heads(v, lanes):
    top, rest = halves(v)
    return dot(top, lanes, 1, 1) + dot(rest, lanes, 1, 1)


def lower_triangle():
    row = lax.broadcasted_iota(jnp.int32, (ROWS, ROWS), 0)
    return row >= lax.broadcasted_iota(jnp.int32, (ROWS, ROWS), 1)


def first_half():
    return lax.broadcasted_iota(jnp.int32, (ROWS, 128), 1) < HEADDIM


def silu_slope(v):
    sig = jax.nn.sigmoid(v)
    return sig * (1.0 + v * (1.0 - sig))


def of_part(t):
    return slice(t * WIDE, (t + 1) * WIDE)


def weights_of(buf, t):
    block = buf[t // 4, t % 4]
    return block.reshape(D, block.shape[-1])


def pair(ref, cols, first):
    both = ref[:, cols]
    zero = jnp.zeros_like(both)
    return jnp.where(first, both, zero), jnp.where(first, zero, both)


def norm_of(x, gain):
    x = x.astype(F32)
    inverse = lax.rsqrt(jnp.mean(x * x, axis=1, keepdims=True) + EPSILON)
    return (x * inverse * gain).astype(BF16)


def pack(buf, whole):
    for k in range(PARTS):
        other, low = 8 + k // 2, k % 2 * 64
        buf[k, :STATE] = whole[:, k * 128 : k * 128 + 128]
        buf[k, STATE : STATE + 64] = whole[low : low + 64, other * 128 : other * 128 + 128]


def unpack(whole, buf):
    for k in range(PARTS):
        other, low = 8 + k // 2, k % 2 * 64
        whole[:, k * 128 : k * 128 + 128] = buf[k, :STATE]
        whole[low : low + 64, other * 128 : other * 128 + 128] = buf[k, STATE : STATE + 64]


def kept_of(s, block):
    rows = s.fresh_in[block, STATE + 64 :].astype(F32)
    first = lax.broadcasted_iota(jnp.int32, (STATE + 64, 128), 0) < STATE
    return jnp.where(first, rows[0:1] + rows[1:2], rows[2:3] + rows[3:4])


def make_blocks(s, me):
    t = me["t"]
    row = lax.broadcasted_iota(jnp.int32, (64, 48), 0)
    given = s.w_step[...].astype(F32)
    steps = jnp.zeros((64, 48), F32)
    for k in range(3):
        steps = jnp.where(row == 3 * t + k, given[k : k + 1], steps)
    s.turned[...] = jnp.zeros_like(s.turned)
    s.turned[:, :48] = steps
    steps = s.turned[...].T[:48].astype(BF16)
    for p in range(3):
        rows = slice(16 * p, 16 * p + 16)
        s.own_v[p, :, :WIDE] = s.w_value[rows]
        s.own_v[p, :, WIDE:] = steps[rows]
        s.own_g[p, :, :WIDE] = s.w_gate[rows]
        s.own_g[p, :, WIDE:] = s.w_out[rows]
    lane = lax.broadcasted_iota(jnp.int32, (1, 256), 1)
    row6, row7 = jnp.zeros((1, 256), F32), jnp.zeros((1, 256), F32)
    for k in range(3):
        row6 = jnp.where(lane == 3 * t + k, s.step_bias[k], row6)
        row6 = jnp.where(lane == 128 + 3 * t + k, s.decay_log[k], row6)
        row7 = jnp.where(lane == 3 * t + k, s.skip_gain[k], row7)
    s.own_p[...] = jnp.zeros_like(s.own_p)
    s.own_p[0:4, :WIDE] = s.conv_inner[...]
    s.own_p[4:5, :WIDE] = s.bias_inner[...].reshape(1, WIDE)
    s.own_p[5:6, :WIDE] = s.out_gain[...].reshape(1, WIDE)
    s.own_p[6:7] = row6
    s.own_p[7:8] = row7


SAME, AFTER, ENDING, JOINED, KEPT, IDS = 0, 3, 7, 8, 9, 10


def segs_of(s, block):
    return s.segs[pl.ds(pl.multiple_of(block * ROWS, ROWS), ROWS)].reshape(1, ROWS).astype(F32)


def make_masks(s, me):
    t = me["t"]
    ids = segs_of(s, t)
    ahead = jnp.where(t > 0, segs_of(s, (t + 7) % PARTS), -1.0)
    later = jnp.where(t < PARTS - 1, segs_of(s, (t + 1) % PARTS), -1.0)
    lane = lax.broadcasted_iota(jnp.int32, (8, ROWS), 1)
    ids8, ahead8, later8 = (jnp.broadcast_to(v, (8, ROWS)) for v in (ids, ahead, later))
    one, zero = jnp.ones((8, ROWS), F32), jnp.zeros((8, ROWS), F32)
    row = lax.broadcasted_iota(jnp.int32, (8, ROWS), 0)
    top, low = zero, zero
    for k in (1, 2, 3):
        shifted = jnp.where(lane < k, pltpu.roll(ahead8, k, 1), pltpu.roll(ids8, k, 1))
        top = jnp.where((row == SAME + k) & (shifted == ids8), one, top)
        shifted = jnp.where(lane >= ROWS - k, pltpu.roll(later8, ROWS - k, 1), pltpu.roll(ids8, ROWS - k, 1))
        top = jnp.where((row == AFTER + k) & (shifted == ids8), one, top)
    last, before = ids8[:, ROWS - 1 :], ahead8[:, ROWS - 1 :]
    top = jnp.where((row == ENDING) & (ids8 == last), one, top)
    low = jnp.where((row == JOINED - 8) & (ids8 == before), one, low)
    low = jnp.where((row == KEPT - 8) & (last == before), one, low)
    low = jnp.where(row == IDS - 8, ids8, low)
    s.masks[...] = jnp.concatenate([top, low, jnp.zeros((112, ROWS), F32)], axis=0).T


def conv_sum(before, taps, bias, masks):
    total = bias + taps[3:4] * before[HALO:]
    for k in (1, 2, 3):
        shifted = before[HALO - k : HALO - k + ROWS]
        total = total + taps[3 - k : 4 - k] * (masks[:, SAME + k : SAME + k + 1] * shifted)
    return total


def enter_shared(s):
    before = dot(s.normed[...], s.w_shared[...], 1, 0)
    s.spre[...] = before
    total = conv_sum(before, s.conv_shared[...], s.bias_shared[...].reshape(1, 2 * STATE), s.masks[...])
    s.ssum[...] = total
    s.bc[...] = (total * jax.nn.sigmoid(total)).astype(BF16)


def enter_value(s, t):
    cols = of_part(t)
    block = s.prm[t]
    before = dot(s.normed[...], weights_of(s.wv, t)[:, :WIDE], 1, 0)
    s.vpre[:, cols] = before
    total = conv_sum(before, block[0:4, :WIDE], block[4:5, :WIDE], s.masks[...])
    s.vsum[:, cols] = total
    s.vals[:, cols] = (total * jax.nn.sigmoid(total)).astype(BF16)


def step_weights(s):
    total = weights_of(s.wv, 0)[:, 128:]
    for t in range(1, PARTS):
        total = total + weights_of(s.wv, t)[:, 128:]
    return total


def enter_step(s):
    heads = s.prm[0, 6:8]
    for t in range(1, PARTS):
        heads = heads + s.prm[t, 6:8]
    is_head = lax.broadcasted_iota(jnp.int32, (ROWS, 128), 1) < HEADS
    s.rate[...] = jnp.where(is_head[0:8], -jnp.exp(jnp.broadcast_to(heads[0:1, 128:], (8, 128))), 0.0)
    s.skip[...] = jnp.broadcast_to(heads[1:2, :128], (8, 128))
    s.wstep[...] = step_weights(s)
    step = dot(s.normed[HALO:], s.wstep[...], 1, 0)
    raw = jnp.where(is_head, pltpu.roll(step, 64, 1) + heads[0:1, :128], 0.0)
    s.raw[...] = raw
    dt = jnp.where(is_head, jnp.maximum(raw, 0.0) + jnp.log1p(jnp.exp(-jnp.abs(raw))), 0.0)
    s.dt[...] = dt
    logs = dot(lower_triangle().astype(F32), dt * s.rate[0:1], 1, 0, HIGHEST)
    s.logs[...] = logs
    s.dt_t[...] = dt.T
    s.logs_t[...] = logs.T


def make_fresh(s):
    logs, masks = s.logs[...], s.masks[...]
    last = logs[ROWS - 1 :]
    top, rest = halves(masks[:, ENDING : ENDING + 1] * jnp.exp(last - logs) * s.dt[...])
    s.weight_top[...] = top
    s.weight_rest[...] = rest

    def body(cols):
        weights = dot(s.weight_top[...], s.lanes[:, cols], 1, 0) + dot(s.weight_rest[...], s.lanes[:, cols], 1, 0)
        weighted = (s.vals[:, cols].astype(F32) * weights).astype(BF16)
        s.state[:, cols] = dot(s.bc[:, :STATE], weighted, 0, 0).astype(BF16)

    columns(body)
    kept = masks[0:8, KEPT : KEPT + 1] * jnp.exp(jnp.broadcast_to(last, (8, 128)))
    top, rest = halves(to_units(kept, s.lanes[...])[0:1])
    top, rest = top.astype(F32), rest.astype(F32)
    pack(s.fresh, s.state)
    row = lax.broadcasted_iota(jnp.int32, (16, 128), 0)
    for k in range(PARTS):
        tail = jnp.zeros((16, 128), F32)
        for at, part, tile in ((0, top, k), (1, rest, k), (2, top, 8 + k // 2), (3, rest, 8 + k // 2)):
            tail = jnp.where(row == at, part[:, tile * 128 : tile * 128 + 128], tail)
        s.fresh[k, STATE + 64 :] = tail.astype(BF16)


def scan_states(s):
    state = jnp.zeros((STATE + 64, 128), F32)
    for b in range(PARTS):
        s.state_out[b] = state.astype(BF16)
        state = s.fresh_in[b, : STATE + 64].astype(F32) + kept_of(s, b) * state


def scan_back(s):
    coming = jnp.zeros((STATE + 64, 128), F32)
    for b in reversed(range(PARTS)):
        s.coming_out[b] = coming.astype(BF16)
        coming = s.dstate_in[b].astype(F32) + kept_of(s, b) * coming


def tiles(low, high, body, width=128):
    def step(tile, carry):
        body(tile, pl.ds(pl.multiple_of(tile * width, width), width))
        return carry

    lax.fori_loop(low, high, step, 0, unroll=6 if width == 256 else 2)


def columns(body):
    tiles(0, INNER // 256, lambda tile, cols: body(cols), 256)


def make_scores(s):
    masks = s.masks[...]
    ids_row = masks.T[IDS : IDS + 1]
    allowed = lower_triangle() & (masks[:, IDS : IDS + 1] == ids_row)
    s.allowed[...] = jnp.where(allowed, 1.0, 0.0)
    s.scores[...] = jnp.where(allowed, dot(s.bc[:, STATE:], s.bc[:, :STATE], 1, 1), 0.0)


def mix_inside(s, low, high):
    def body(tile, cols):
        logs = pltpu.roll(s.logs[...], (128 - 2 * tile) % 128, 1)
        total = jnp.zeros((ROWS, 128), F32)
        for j, vals in enumerate(pair(s.vals, cols, first_half())):
            h = 2 * tile + j
            gaps = jnp.minimum(logs[:, j : j + 1] - s.logs_t[pl.ds(h, 1), :], 0.0)
            decay = (jnp.exp(gaps) * s.dt_t[pl.ds(h, 1), :]).astype(BF16)
            s.dec[h] = decay
            mix = (s.scores[...] * decay.astype(F32)).astype(BF16)
            total = total + dot(mix, vals, 1, 0)
        s.inner[:, cols] = total

    tiles(low, high, body)


def add_states(s):
    top, rest = halves(s.masks[:, JOINED : JOINED + 1] * jnp.exp(s.logs[...]))
    s.weight_top2[...] = top
    s.weight_rest2[...] = rest
    unpack(s.state, s.state_in)
    s.skips[...] = to_units(s.skip[...], s.lanes[...])
    s.squares[...] = jnp.zeros_like(s.squares)

    def body(cols):
        carried = dot(s.weight_top2[...], s.lanes[:, cols], 1, 0) + dot(s.weight_rest2[...], s.lanes[:, cols], 1, 0)
        inner = s.inner[:, cols] + dot(s.bc[:, STATE:], s.state[:, cols], 1, 0) * carried
        s.inner[:, cols] = inner
        gate = s.gate[:, cols]
        gated = (inner + s.skips[0:1, cols] * s.vals[:, cols].astype(F32)) * (gate * jax.nn.sigmoid(gate))
        s.normal[:, cols] = gated
        s.squares[...] = s.squares[...] + gated * gated

    columns(body)


def gated_norm(s):
    inverse = lax.rsqrt(jnp.sum(s.squares[...], axis=1, keepdims=True) / INNER + EPSILON)
    s.inverse[...] = jnp.broadcast_to(inverse, (ROWS, 128))
    for t in range(PARTS):
        s.gain_out[:, of_part(t)] = jnp.broadcast_to(s.prm[t, 5:6, :WIDE], (8, WIDE))
    s.squares[...] = jnp.zeros_like(s.squares)

    def body(cols):
        normal = s.normal[:, cols] * s.inverse[:, 0:1]
        s.normal[:, cols] = normal
        gain = s.gain_out[0:1, cols]
        s.nout[:, cols] = (normal * gain).astype(BF16)
        d_out = s.dout[:, cols]
        product = d_out * normal
        s.small[5:6, cols] = jnp.sum(product, axis=0, keepdims=True)
        s.squares[...] = s.squares[...] + product * gain

    columns(body)


def project_back(s, t):
    cols = of_part(t)
    s.dout[:, cols] = dot(s.cot[...], weights_of(s.wg, t)[:, WIDE:], 1, 0)


def project_out(s):
    branch = s.x[...].astype(F32)
    for t in range(PARTS):
        branch = branch + dot(s.nout[:, of_part(t)], weights_of(s.wg, t)[:, WIDE:], 1, 1)
    s.result_in[...] = branch.astype(BF16)


def gated_norm_back(s):
    total = jnp.sum(s.squares[...], axis=1, keepdims=True) / INNER
    s.dots[...] = jnp.broadcast_to(total, (ROWS, 128))

    def body(cols):
        d_scaled = s.dout[:, cols] * s.gain_out[0:1, cols]
        d_gated = s.inverse[:, 0:1] * (d_scaled - s.normal[:, cols] * s.dots[:, 0:1])
        gate = s.gate[:, cols]
        sig = jax.nn.sigmoid(gate)
        vals = s.vals[:, cols].astype(F32)
        mixed = s.inner[:, cols] + s.skips[0:1, cols] * vals
        d_mixed = d_gated * (gate * sig)
        s.dgate[:, cols] = (d_gated * mixed * sig * (1.0 + gate * (1.0 - sig))).astype(BF16)
        s.small[6:7, cols] = jnp.sum(d_mixed * vals, axis=0, keepdims=True)
        s.dy[:, cols] = d_mixed.astype(BF16)
        s.dval[:, cols] = s.skips[0:1, cols] * d_mixed
        lanes = s.lanes[:, cols]
        carried = dot(s.weight_top2[...], lanes, 1, 0) + dot(s.weight_rest2[...], lanes, 1, 0)
        d_carried = (d_mixed * carried).astype(BF16)
        s.dcar[:, cols] = d_carried
        s.dfresh[:, cols] = dot(s.bc[:, STATE:], d_carried, 0, 0).astype(BF16)

    columns(body)


def states_back(s):
    pack(s.dstate, s.dfresh)


def mix_back(s, low, high):
    def body(tile, cols):
        total = jnp.zeros((ROWS, 128), F32)
        d_scores = s.dscores[...]
        first = first_half()
        for j, (vals, grads) in enumerate(zip(pair(s.vals, cols, first), pair(s.dy, cols, first))):
            h = 2 * tile + j
            d_mix = dot(grads, vals, 1, 1)
            decay = s.dec[h].astype(F32)
            d_scores = d_scores + d_mix * decay
            total = total + dot((s.scores[...] * decay).astype(BF16), grads, 0, 0)
        s.dscores[...] = d_scores
        s.dval[:, cols] = s.dval[:, cols] + total
        s.dout[:, cols] = total * s.vals[:, cols].astype(F32)

    tiles(low, high, body)


def after_mix_back(s):
    s.direct[...] = jnp.zeros_like(s.direct)
    s.dlog[...] = jnp.zeros_like(s.dlog)

    def body(cols):
        lanes = s.lanes[:, cols]
        from_values = s.dout[:, cols]
        s.direct[...] = s.direct[...] + to_heads(from_values, lanes)
        s.dlog[...] = s.dlog[...] + to_heads(s.dy[:, cols].astype(F32) * s.inner[:, cols] - from_values, lanes)

    columns(body)
    d_scores = (s.dscores[...] * s.allowed[...]).astype(BF16)
    s.dbc[:, :STATE] = dot(d_scores, s.bc[:, STATE:], 0, 0)
    s.dbc[:, STATE:] = dot(d_scores, s.bc[:, :STATE], 1, 0) + dot(s.dcar[...], s.state[...], 1, 1)


def leave(s):
    lanes = s.lanes[...]
    logs, dt, raw, masks = s.logs[...], s.dt[...], s.raw[...], s.masks[...]
    unpack(s.coming, s.coming_in)
    last = logs[ROWS - 1 :]
    s.through[...] = jnp.zeros_like(s.through)

    def body(cols):
        lanes = s.lanes[:, cols]
        weights = dot(s.weight_top[...], lanes, 1, 0) + dot(s.weight_rest[...], lanes, 1, 0)
        weighted = s.vals[:, cols].astype(F32) * weights
        below = dot(s.bc[:, :STATE], s.coming[:, cols], 1, 0)
        s.dsum[:ROWS, cols] = (s.dval[:, cols] + weights * below) * silu_slope(s.vsum[:, cols])
        s.through[...] = s.through[...] + to_heads(weighted * below, lanes)
        s.dbc[:, :STATE] = s.dbc[:, :STATE] + dot(weighted.astype(BF16), s.coming[:, cols], 1, 1)

    columns(body)
    through, coming = s.through[...], s.coming[...]
    kept = masks[0:8, KEPT : KEPT + 1] * jnp.exp(jnp.broadcast_to(last, (8, 128)))
    held = jnp.sum(coming.astype(F32) * s.state[...].astype(F32), axis=0, keepdims=True)
    d_kept = to_heads(jnp.broadcast_to(held, (8, INNER)), lanes)
    d_last = jnp.sum(through, axis=0, keepdims=True) + (d_kept * kept)[0:1]
    row = lax.broadcasted_iota(jnp.int32, (ROWS, ROWS), 0)
    upper = row <= lax.broadcasted_iota(jnp.int32, (ROWS, ROWS), 1)
    d_rate = dot(upper.astype(F32), s.dlog[...] - through, 1, 0, HIGHEST) + d_last
    by_rate = dt * s.rate[0:1] * d_rate
    slope = jnp.where(raw < -15.0, 1.0, jax.nn.sigmoid(raw) / jnp.where(raw < -15.0, 1.0, dt))
    is_head = lax.broadcasted_iota(jnp.int32, (ROWS, 128), 1) < HEADS
    d_step = jnp.where(is_head, (s.direct[...] + through + by_rate) * slope, 0.0)
    s.dstep[...] = d_step.astype(BF16)
    s.small[7:8, 0:128] = jnp.sum(d_step, axis=0, keepdims=True)
    s.small[7:8, 128:256] = jnp.sum(by_rate, axis=0, keepdims=True)
    s.dsum[:ROWS, INNER:] = s.dbc[...] * silu_slope(s.ssum[...])
    s.edge[...] = s.dsum[0:8]


def conv_grads(s):
    masks = s.masks[...]

    def rows_of(d_sum, before_ref, cols):
        rows = []
        for k in (3, 2, 1):
            shifted = masks[:, SAME + k : SAME + k + 1] * before_ref[HALO - k : HALO - k + ROWS, cols]
            rows.append(jnp.sum(d_sum * shifted, axis=0, keepdims=True))
        rows.append(jnp.sum(d_sum * before_ref[HALO:, cols], axis=0, keepdims=True))
        rows.append(jnp.sum(d_sum, axis=0, keepdims=True))
        return rows

    def body(cols):
        for k, row in enumerate(rows_of(s.dsum[:ROWS, cols], s.vpre, cols)):
            s.small[k : k + 1, cols] = row

    columns(body)
    for k, row in enumerate(rows_of(s.dsum[:ROWS, INNER:], s.spre, EVERY)):
        s.small[7:8, 256 * (k + 1) : 256 * (k + 2)] = row


def conv_back(s):
    masks = s.masks[...]

    def back(cols, taps):
        total = taps[3:4] * s.dsum[:ROWS, cols]
        for k in (1, 2, 3):
            ahead = masks[:, AFTER + k : AFTER + k + 1] * s.dsum[k : k + ROWS, cols]
            total = total + taps[3 - k : 4 - k] * ahead
        return total.astype(BF16)

    for t in range(PARTS):
        cols = of_part(t)
        s.dvlow[:, cols] = back(cols, s.prm[t, 0:4, :WIDE])
    s.dshared[...] = back(slice(INNER, INNER + 2 * STATE), s.conv_shared[...])


def as_block(v):
    return v.reshape(4, 2, 2, 3, 16, v.shape[-1])


def parts_g(s, t):
    cols = of_part(t)
    gates = dot(s.normed_t[...], s.dgate[:, cols], 1, 0)
    outs = dot(s.cot_t[...], s.nout[:, cols], 1, 0)
    s.pg[t // 4, t % 4] = as_block(jnp.concatenate([gates, outs], axis=1).astype(BF16))


def parts_shared(s):
    shared = dot(s.normed_t[...], s.dshared[...], 1, 0)
    blank = jnp.zeros((4, 128), F32)
    for k in range(128):
        strip = shared[k // 2 * 12 : k // 2 * 12 + 12, k % 2 * 128 : k % 2 * 128 + 128]
        s.ps[k // 32, k // 16 % 2, k // 8 % 2, k % 8] = jnp.concatenate([strip, blank], axis=0).astype(BF16)


def parts_v(s):
    steps = dot(s.normed_t[...], s.dstep[...], 1, 0)[:, :64].astype(BF16)
    for t in range(PARTS):
        values = dot(s.normed_t[...], s.dvlow[:, of_part(t)], 1, 0).astype(BF16)
        s.pv[t // 4, t % 4] = as_block(jnp.concatenate([values, steps], axis=1))


def normed_back_g(s):
    total = jnp.zeros((ROWS, D), F32)
    for t in range(PARTS):
        total = total + dot(s.dgate[:, of_part(t)], weights_of(s.wg, t)[:, :WIDE], 1, 1)
    s.dnormed[...] = total


def normed_back_v(s):
    total = s.dnormed[...] + dot(s.dshared[...], s.w_shared[...], 1, 1)
    total = total + dot(pltpu.roll(s.dstep[...].astype(F32), 64, 1).astype(BF16), s.wstep[...], 1, 1)
    for t in range(PARTS):
        total = total + dot(s.dvlow[:, of_part(t)], weights_of(s.wv, t)[:, :WIDE], 1, 1)
    x = s.x[...].astype(F32)
    inverse = lax.rsqrt(jnp.mean(x * x, axis=1, keepdims=True) + EPSILON)
    scaled = x * inverse
    d_in = total * s.in_gain[...].reshape(1, D)
    gains = jnp.sum(total * scaled, axis=0, keepdims=True)
    s.gain_row[...] = jnp.zeros_like(s.gain_row)
    for k in range(D // 128):
        s.gain_row[k : k + 1] = gains[:, k * 128 : k * 128 + 128]
    centred = jnp.mean(d_in * scaled, axis=1, keepdims=True)
    s.resid_in[...] = inverse * (d_in - scaled * centred) + s.cot[...].astype(F32)


def own_part(row, me, width):
    total = jnp.where(me["t"] == 0, row[:, :width], 0.0)
    for t in range(1, PARTS):
        total = total + jnp.where(me["t"] == t, row[:, t * width : (t + 1) * width], 0.0)
    return total


def closing_kernel(*refs):
    names = [*RESULTS, *OUTPUTS]
    s = types.SimpleNamespace(**dict(zip(names, refs)))
    me = place()
    s.result[...] = s.result_in[...]
    s.grad_resid[...] = s.resid_in[...]
    s.grad_w_value[...] = s.block_v[:, :WIDE]
    steps = s.block_v[:, 128:].T
    s.grad_w_step[...] = sum(jnp.where(me["t"] == t, steps[64 + 3 * t : 67 + 3 * t], 0.0) for t in range(PARTS))
    s.grad_w_gate[...] = s.block_g[:, :WIDE]
    s.grad_w_out[...] = s.block_g[:, WIDE:]
    total = s.total[...]
    own = own_part(total, me, WIDE)
    s.grad_conv_inner[...] = own[0:4]
    s.grad_bias_inner[...] = own[4:5].reshape(WIDE)
    s.grad_out_gain[...] = own[5:6].reshape(WIDE)
    for k in range(4):
        s.grad_conv_shared[k : k + 1] = total[7:8, 256 * (k + 1) : 256 * (k + 2)]
    s.grad_bias_shared[...] = total[7:8, 1280:].reshape(2 * STATE)
    s.grad_step_bias[...] = own_part(total[7:8, 0:24], me, 3)
    s.grad_decay_log[...] = own_part(total[7:8, 128:152], me, 3)
    s.grad_skip_gain[...] = own_part(to_heads(total, head_lanes())[6:7, 0:24], me, 3)
    for k in range(D // 128):
        s.grad_in_gain[k * 128 : k * 128 + 128] = s.gains[k]
    for k in range(128):
        tile = s.tails_in[k // 32, k // 16 % 2, k // 8 % 2, k % 8].astype(F32)
        s.grad_w_shared[k // 2 * 12 : k // 2 * 12 + 12, k % 2 * 128 : k % 2 * 128 + 128] = tile[:12]


INPUTS = dict(
    x=0, cot=0, segs=0, in_gain=0, w_gate=0, w_value=0, w_step=0, w_shared=0, conv_inner=0, bias_inner=0,
    conv_shared=0, bias_shared=0, step_bias=1, decay_log=1, skip_gain=1, out_gain=0, w_out=0,
)
OUTPUTS = dict(
    result=((ROWS, D), BF16), grad_resid=((ROWS, D), F32), grad_in_gain=((D,), F32),
    grad_w_gate=((48, WIDE), F32), grad_w_value=((48, WIDE), F32), grad_w_step=((3, 48), F32),
    grad_w_shared=((D, 2 * STATE), F32), grad_conv_inner=((4, WIDE), F32), grad_bias_inner=((WIDE,), F32),
    grad_conv_shared=((4, 2 * STATE), F32), grad_bias_shared=((2 * STATE,), F32),
    grad_step_bias=((1, 3), F32), grad_decay_log=((1, 3), F32), grad_skip_gain=((1, 3), F32),
    grad_out_gain=((WIDE,), F32), grad_w_out=((48, WIDE), F32),
)
RESULTS = dict(
    result_in=((ROWS, D), BF16), resid_in=((ROWS, D), F32), block_v=((48, PACK_V), F32),
    block_g=((48, PACK_G), F32), total=((8, INNER), F32), gains=((8, 128), F32),
    tails_in=((4, 2, 2, 8, 16, 128), BF16),
)
TORUS = (2, 4, 4, 2, 2, 3, 16)


def reduce_scratch(width, relayed, orders):
    block = (16, width)
    last = [free_shape(order[2:]) + block for order in orders]
    half = [free_shape(order[2:], True) + block for order in orders]
    line = [free_shape(order[1:]) + block for order in orders]
    kinds = [(4, last), (2 if relayed else 3, last), (3, line)]
    shapes = [(lead,) + shape for lead, shapes in kinds for shape in shapes] + [(3, 3) + block]
    return shapes + ([(2,) + shape for shape in half] if relayed else [])


SCRATCH = dict(
    wv=(TORUS + (PACK_V,), BF16), wg=(TORUS + (PACK_G,), BF16),
    pv=(TORUS + (PACK_V,), BF16), pg=(TORUS + (PACK_G,), BF16), ps=((4, 2, 2, 8, 16, 128), BF16), heard_s=((4, 2, 8, 16, 128), BF16),
    got_s=((64, 16, 128), BF16),
    own_v=((3, 16, PACK_V), BF16), own_g=((3, 16, PACK_G), BF16), own_t=((16, 128), BF16), turned=((64, 128), F32),
    own_p=((8, 256), F32), prm=((PARTS, 8, 256), F32), ahead=((HALO, D), BF16),
    normed=((HALO + ROWS, D), BF16), normed_t=((D, ROWS), BF16), cot_t=((D, ROWS), BF16),
    masks=((ROWS, 128), F32), lanes=((128, INNER), BF16), dfresh=((STATE, INNER), BF16),
    weight_top=((ROWS, 128), BF16), weight_rest=((ROWS, 128), BF16), through=((ROWS, 128), F32),
    weight_top2=((ROWS, 128), BF16), weight_rest2=((ROWS, 128), BF16), dots=((ROWS, 128), F32),
    squares=((ROWS, 256), F32),
    vpre=((HALO + ROWS, INNER), F32), vsum=((ROWS, INNER), F32), vals=((ROWS, INNER), BF16),
    spre=((HALO + ROWS, 256), F32), ssum=((ROWS, 256), F32), bc=((ROWS, 256), BF16),
    rate=((8, 128), F32), skip=((8, 128), F32), skips=((8, INNER), F32), gain_out=((8, INNER), F32),
    wstep=((D, 128), BF16), raw=((ROWS, 128), F32), dt=((ROWS, 128), F32), logs=((ROWS, 128), F32),
    dt_t=((128, ROWS), F32), logs_t=((128, ROWS), F32),
    fresh=((PARTS, 208, 128), BF16), fresh_in=((PARTS, 208, 128), BF16),
    state_out=((PARTS, STATE + 64, 128), BF16), state_in=((PARTS, STATE + 64, 128), BF16),
    dstate=((PARTS, STATE + 64, 128), BF16), dstate_in=((PARTS, STATE + 64, 128), BF16),
    coming_out=((PARTS, STATE + 64, 128), BF16), coming_in=((PARTS, STATE + 64, 128), BF16),
    state=((STATE, INNER), BF16),
    scores=((ROWS, ROWS), F32), dscores=((ROWS, ROWS), F32), allowed=((ROWS, ROWS), F32),
    dec=((HEADS, ROWS, ROWS), BF16),
    inner=((ROWS, INNER), F32),
    gate=((ROWS, INNER), F32), normal=((ROWS, INNER), F32),
    inverse=((ROWS, 128), F32), nout=((ROWS, INNER), BF16), dout=((ROWS, INNER), F32),
    dgate=((ROWS, INNER), BF16), dy=((ROWS, INNER), BF16), dcar=((ROWS, INNER), BF16),
    direct=((ROWS, 128), F32), dlog=((ROWS, 128), F32),
    dbc=((ROWS, 256), F32), dstep=((ROWS, 128), BF16),
    dsum=((ROWS + 8, INNER + 256), F32), edge=((8, INNER + 256), F32),
    dshared=((ROWS, 256), BF16),
    small=((8, INNER), F32), small_sums=((4, 8, INNER), F32), small_got=((10, 8, INNER), F32),
    gain_row=((8, 128), F32), gain_sums=((4, 8, 128), F32), gain_got=((10, 8, 128), F32),
)
SEMAPHORES = dict(
    gather_v=45, gather_g=45, shared=4, reduce_g=42, reduce_v=42,
    total=10, total_gain=10, swap_p=8, swap1=8, swap2=8, swap3=8, swap4=8, edges=2,
)


def reducer(me, orders, parts, refs, sems):
    return Reduce(me, orders, parts, refs[0:3], refs[10:13] or None, refs[3:6], refs[6:9], refs[9], sems)


REDUCE_G = reduce_scratch(PACK_G, True, ASIDE)
REDUCE_V = reduce_scratch(PACK_V, False, ORDERS)


def everything(s, sems):
    me = place()
    dp, t = me["dp"], me["t"]
    after, before = (dp, (t + 1) % PARTS), (dp, (t + 7) % PARTS)
    greet(me)
    make_blocks(s, me)
    in_gain = s.in_gain[...].reshape(1, D)
    s.normed[HALO:] = norm_of(s.x[...], in_gain)
    make_masks(s, me)
    greeted()

    gather_v = Gather(me, s.own_v, s.wv, sems.gather_v, False)
    gather_g = Gather(me, s.own_g, s.wg, sems.gather_g, True)
    gather_v.first()
    halo = transfer(s.x.at[pl.ds(ROWS - HALO, HALO)], s.ahead, sems.edges, 0, after)
    gather_g.first()
    params = [transfer(s.own_p, s.prm.at[t], sems.swap_p, by, (dp, (t + by) % PARTS)) for by in range(1, PARTS)]
    s.prm[t] = s.own_p[...]
    s.lanes[...] = head_lanes()
    gather_v.second()
    halo.wait_recv()
    s.normed[:HALO] = norm_of(s.ahead[...], in_gain)
    gather_v.third()
    gather_g.second()
    enter_shared(s)
    make_scores(s)
    s.normed_t[...] = s.normed[HALO:].T
    s.cot_t[...] = s.cot[...].T
    for copy in params:
        copy.wait_recv()
    gather_v.relay()
    gather_v.finish()
    gather_g.third()
    gather_v.settle()

    enter_step(s)
    for part in range(PARTS):
        enter_value(s, part)
    make_fresh(s)
    swap1 = Swap(me, s.fresh, s.fresh_in, sems.swap1)
    swap1.start()
    gather_g.relay()
    mix_inside(s, 0, 8)
    swap1.wait()
    scan_states(s)
    swap2 = Swap(me, s.state_out, s.state_in, sems.swap2)
    swap2.start()
    gather_g.finish()
    mix_inside(s, 8, 12)
    gather_g.settle()
    for part in range(PARTS):
        s.gate[:, of_part(part)] = dot(s.normed[HALO:], weights_of(s.wg, part)[:, :WIDE], 1, 0)
        project_back(s, part)
    swap2.wait()
    add_states(s)
    gated_norm(s)
    gated_norm_back(s)
    states_back(s)
    swap3 = Swap(me, s.dstate, s.dstate_in, sems.swap3)
    swap3.start()
    for part in range(PARTS):
        parts_g(s, part)
    reduce_g = reducer(me, ASIDE, s.pg, s.refs_g, sems.reduce_g)
    reduce_g.swap()
    s.dscores[...] = jnp.zeros_like(s.dscores)
    project_out(s)
    mix_back(s, 0, 2)
    reduce_g.relay()
    mix_back(s, 2, 6)
    swap3.wait()
    scan_back(s)
    swap4 = Swap(me, s.coming_out, s.coming_in, sems.swap4)
    swap4.start()
    mix_back(s, 6, 8)
    reduce_g.third()
    mix_back(s, 8, 12)
    after_mix_back(s)
    normed_back_g(s)
    swap4.wait()
    leave(s)
    edge = transfer(s.edge, s.dsum.at[pl.ds(ROWS, 8)], sems.edges, 1, before)
    conv_grads(s)
    total = Total(me, s.small, s.small_sums, s.small_got, sems.total)
    total.along(0)
    reduce_g.second()
    edge.wait_recv()
    conv_back(s)
    parts_shared(s)
    shared = Shared(me, s.ps, s.heard_s, s.got_s, s.own_t, s.tails_in, sems.shared)
    shared.swap()
    parts_v(s)
    reduce_v = reducer(me, ORDERS, s.pv, s.refs_v, sems.reduce_v)
    reduce_v.swap()
    shared.scatter()
    reduce_v.relay()
    reduce_v.third()
    total.add(0)
    total.along(1)
    normed_back_v(s)
    gain = Total(me, s.gain_row, s.gain_sums, s.gain_got, sems.total_gain)
    gain.along(0)
    reduce_g.first()
    shared.gather()
    gain.add(0)
    gain.along(1)
    reduce_v.second()
    total.add(1)
    total.along(2)
    gain.add(1)
    gain.along(2)
    reduce_v.first()
    total.add(2)
    total.along(3)
    gain.add(2)
    gain.along(3)
    shared.share()
    for p in range(3):
        s.block_g[16 * p : 16 * p + 16] = reduce_g.result(p)
    for p in range(3):
        s.block_v[16 * p : 16 * p + 16] = reduce_v.result(p)
    total.add(3)
    s.total[...] = s.small_sums[3]
    gain.add(3)
    s.gains[...] = s.gain_sums[3]
    shared.finish()

    for channel in (gather_v, gather_g, shared, reduce_g, reduce_v, total, gain, swap1, swap2, swap3, swap4):
        channel.drain()
    for copy in [halo, edge, *params]:
        copy.wait_send()


def kernel(*refs):
    tables = (INPUTS, RESULTS, SCRATCH)
    names = [name for table in tables for name in table]
    s = types.SimpleNamespace(**dict(zip(names, refs)))
    s.dval, s.dvlow = s.normal, s.dy
    s.dnormed, s.coming = s.gate.at[:, :D], s.dcar.at[:STATE]
    at = len(names)
    s.refs_g, at = refs[at : at + len(REDUCE_G)], at + len(REDUCE_G)
    s.refs_v, at = refs[at : at + len(REDUCE_V)], at + len(REDUCE_V)
    pairs = zip(refs[at::2], refs[at + 1 :: 2])
    everything(s, types.SimpleNamespace(**dict(zip(SEMAPHORES, pairs))))


def shards(*args):
    args = list(args)
    args[6] = args[6].T
    vmem, smem = pl.BlockSpec(memory_space=pltpu.VMEM), pl.BlockSpec(memory_space=pltpu.SMEM)
    scratch = [pltpu.VMEM(shape, dtype) for shape, dtype in SCRATCH.values()]
    scratch += [pltpu.VMEM(shape, BF16) for shape in REDUCE_G + REDUCE_V]
    for count in SEMAPHORES.values():
        scratch += [pltpu.SemaphoreType.DMA((count,)), pltpu.SemaphoreType.DMA((count,))]
    shapes = lambda table: tuple(jax.ShapeDtypeStruct(shape, dtype) for shape, dtype in table.values())
    results = pl.pallas_call(
        kernel,
        out_shape=shapes(RESULTS),
        in_specs=[smem if scalar else vmem for scalar in INPUTS.values()],
        out_specs=tuple(vmem for _ in RESULTS),
        scratch_shapes=scratch,
        compiler_params=pltpu.CompilerParams(
            collective_id=0, has_side_effects=True, vmem_limit_bytes=VMEM_LIMIT
        ),
    )(*args)
    outs = pl.pallas_call(
        closing_kernel,
        out_shape=shapes(OUTPUTS),
        in_specs=[vmem for _ in RESULTS],
        out_specs=tuple(vmem for _ in OUTPUTS),
    )(*results)
    outs = [out.reshape(3) if out.shape == (1, 3) else out for out in outs]
    outs[5] = outs[5].T
    return tuple(outs)


def solution(mesh):
    rows, cols = P(("dp", "tensor"), None), P("dp", "tensor")
    head, whole = P("tensor"), P()
    in_specs = (
        rows, rows, P("dp"), whole, cols, cols, cols, whole, P(None, "tensor"), head,
        whole, whole, head, head, head, head, cols,
    )
    out_specs = (
        rows, rows, whole, cols, cols, cols, whole, P(None, "tensor"), head,
        whole, whole, head, head, head, head, cols,
    )
    return jax.shard_map(shards, mesh=mesh, in_specs=in_specs, out_specs=out_specs, check_vma=False)
```

time: 864 us -> 109 us (0.13)
  local copies, waits for them, and re-layouts: 225 us -> 0 us
  matrix products: 172 us -> 0 us
  blocking collectives: 153 us -> 0 us
  other arithmetic: 131 us -> 0 us
  Pallas kernels: 0 us -> 106 us
  waiting for transfers between devices: 100 us -> 0 us
  starting transfers between devices: 34.9 us -> 0 us
  loops' own time: 22.6 us -> 0 us
  between operations: 15.6 us -> 0.84 us
    dot_general x111 -> x0, matrix products: 159 us -> none  [the longest x24 46.9 us: advance(): inside = jnp.einsum('hts,shp->thp', mixing, vals, precision=HIGHEST)]
    dynamic_update_slice x48 -> x0, local copies, waits for them, and re-layouts: 106 us -> none  [block_scan(): lax.scan(jax.checkpoint(advance), start, (split(values), split(bees), spl...]
    pallas_call x0 -> x2, Pallas kernels: none -> 106 us  [the longest x1 103 us: shards(): pl.pallas_call(kernel, out_shape=shapes(RESULTS), in_specs=[smem if scala...]
    psum x1 -> x0, waiting for transfers between devices: 74.2 us -> none  [shards(): lax.psum((shared_weight_part, in_gain_part, g_conv_shared, g_bias_shared)...]
    all_gather x2 -> x0, blocking collectives: 72.3 us -> none  [the longest x1 37.2 us: side_by_side(): lax.all_gather(both, axis, axis=dim, tiled=True)]
    psum x1 -> x0, blocking collectives: 71.9 us -> none  [shards(): lax.psum((shared_weight_part, in_gain_part, g_conv_shared, g_bias_shared)...]
    another operation x57 -> x0, other arithmetic: 45.7 us -> none
    all_to_all x7 -> x0, starting transfers between devices: 34.3 us -> none  [the longest x2 13.7 us: copy_for_each(): lax.all_to_all(jnp.broadcast_to(value[None], (length, *value.shape)), axi...]
  transfers between devices with their start and end apart: 13 -> 0, of which waited for: 7 -> 0; matrix products, arithmetic and copies ran while one was open for 61% -> 0% of each run, Pallas kernels for 0% -> 0%
where the time goes in v2:
time: 109 us; the launch traced here: 107 us
  Pallas kernels  106 us (97%)
    pallas_call x1, Pallas kernels, shards(): pl.pallas_call(kernel, out_shape=shapes(RESULTS), in_specs=[smem if scala...  103 us
    pallas_call x1, Pallas kernels, shards(): pl.pallas_call(closing_kernel, out_shape=shapes(OUTPUTS), in_specs=[vmem...  3.18 us

profile of v2, /device:TPU:1, one launch (start us, length us, event | category | flops | bytes accessed | tf_op | source)
XLA Modules:
  0.0 106.5 jit_solution(10474711045655943317)
XLA Ops:
  0.7 102.5 %shard_map.288 = (bf16[256,768]{1,0:T(8,128)(2,1)}, f32[256,768]{1,0:T(8,128)}, f32[48,256]{1,0:T(8,128)}, f32[48,384]{1,0:T(8,128)}, f32[8,1536]{1,0:T(8,128)},...) custom-call(bf16[256,768]{1,0:T(8,128)(2,1)} %refs_0_.1, bf16[256,768]{1,0:T(8,128)(2,1)} %refs_1_.1, ...), custom_call_target="tpu_custom_call" | custom-call | tf_op jit(solution)/shard_map/pallas_call | solution.py:1193
  103.2 3.2 %shard_map.289 = (bf16[256,768]{1,0:T(8,128)(2,1)}, f32[256,768]{1,0:T(8,128)}, f32[768]{0:T(1024)}, f32[48,192]{1,0:T(8,128)}, f32[48,192]{1,0:T(8,128)}, /*ind...) custom-call(bf16[256,768]{1,0:T(8,128)(2,1)} %get-tuple-element.39.r, ...), custom_call_target="tpu_custom_call" | custom-call | tf_op jit(solution)/shard_map/pallas_call | solution.py:1203

commit v3 on v2

--- a/solution.py
+++ b/solution.py
@@ -31,18 +31,26 @@
 EVERY = slice(None)
 
 
+def over(a, n):
+    return lax.div(a, jnp.int32(n))
+
+
+def rest_of(a, n):
+    return lax.rem(a, jnp.int32(n))
+
+
 def place():
     dp, tensor = lax.axis_index("dp"), lax.axis_index("tensor")
-    x = (dp // 2 % 2) * 2 + tensor // 4
-    return {"x": x, "y": tensor % 4, "z": dp // 4, "core": dp % 2, "dp": dp, "t": tensor}
+    x = rest_of(over(dp, 2), 2) * 2 + over(tensor, 4)
+    return {"x": x, "y": rest_of(tensor, 4), "z": over(dp, 4), "core": rest_of(dp, 2), "dp": dp, "t": tensor}
 
 
 def device_of(at):
-    return (at["z"] * 4 + (at["x"] // 2) * 2 + at["core"], (at["x"] % 2) * 4 + at["y"])
+    return (at["z"] * 4 + over(at["x"], 2) * 2 + at["core"], rest_of(at["x"], 2) * 4 + at["y"])
 
 
 def moved(me, dim, by):
-    return {**me, dim: (me[dim] + by) % 4}
+    return {**me, dim: rest_of(me[dim] + by, 4)}
 
 
 def sibling(me):
@@ -50,7 +58,7 @@
 
 
 def region(fixed, half=None):
-    x_lo, x_hi = (fixed["x"] % 2, fixed["x"] // 2) if "x" in fixed else (EVERY, EVERY)
+    x_lo, x_hi = (rest_of(fixed["x"], 2), over(fixed["x"], 2)) if "x" in fixed else (EVERY, EVERY)
     y, z = fixed.get("y", EVERY), fixed.get("z", EVERY)
     if half is not None:
         if "x" not in fixed:
@@ -85,8 +93,8 @@
 
 
 def peer(me, step):
-    z_x = (me["z"] * 2 + me["x"] // 2 + step // 8) % 8
-    return (z_x * 2 + me["core"], (me["t"] + step % 8) % 8)
+    z_x = rest_of(me["z"] * 2 + over(me["x"], 2) + over(step, 8), 8)
+    return (z_x * 2 + me["core"], rest_of(me["t"] + rest_of(step, 8), 8))
 
 
 def each_peer(body):
@@ -172,7 +180,7 @@
             dim = ORDERS[p][2]
             for step, by, half in ((1, 1, 0), (3, 3, 1)):
                 self.got[("c", by), p].wait_recv()
-                value = (me[dim] - by) % 4
+                value = rest_of(me[dim] + 4 - by, 4)
                 if self.relayed:
                     self.go(("r", half), p, 8 + half, self.unit(p, 2, value, half), moved(me, dim, by))
                 self.across(p, 11 + half, value)
@@ -180,7 +188,7 @@
     def finish(self):
         me = self.me
         for p in range(3):
-            across = (me[ORDERS[p][2]] + 2) % 4
+            across = rest_of(me[ORDERS[p][2]] + 2, 4)
             if self.relayed:
                 for half in (0, 1):
                     self.got[("r", half), p].wait_recv()
@@ -197,6 +205,7 @@
     def drain(self):
         for copy in self.sent:
             copy.wait_send()
+        self.sent = []
 
 
 class Reduce:
@@ -208,7 +217,7 @@
     def unit(self, p, stage, by, half=None):
         order = self.orders[p]
         fixed = {dim: self.me[dim] for dim in order[stage + 1 :]}
-        fixed[order[stage]] = (self.me[order[stage]] + by) % 4
+        fixed[order[stage]] = rest_of(self.me[order[stage]] + by, 4)
         return region(fixed, half)
 
     def mine(self, p, stage, by, half=None):
@@ -293,6 +302,7 @@
     def drain(self):
         for copy in self.sent:
             copy.wait_send()
+        self.sent = []
 
 
 class Total:
@@ -323,6 +333,7 @@
     def drain(self):
         for copy in self.sent:
             copy.wait_send()
+        self.sent = []
 
 
 class Shared:
@@ -332,7 +343,7 @@
         self.sent = []
 
     def at(self, device):
-        return (device[0] // 4, device[0] // 2 % 2, device[0] % 2, device[1])
+        return (over(device[0], 4), rest_of(over(device[0], 2), 2), rest_of(device[0], 2), device[1])
 
     def here(self):
         return self.at((self.me["dp"], self.me["t"]))
@@ -401,7 +412,7 @@
     def start(self):
         dp, t = self.me["dp"], self.me["t"]
         for by in (4, 2, 6, 1, 7, 3, 5):
-            to = (t + by) % PARTS
+            to = rest_of(t + by, PARTS)
             self.copies.append(transfer(self.src.at[to], self.got.at[t], self.sems, by, (dp, to)))
         self.got[t] = self.src[t]
 
@@ -412,6 +423,7 @@
     def drain(self):
         for copy in self.copies:
             copy.wait_send()
+        self.copies = []
 
 
 def dot(a, b, over_a, over_b, precision=None):
@@ -669,19 +681,45 @@
 
 
 def mix_inside(s, low, high):
+    half = ROWS // 2
+
     def body(tile, cols):
         logs = pltpu.roll(s.logs[...], (128 - 2 * tile) % 128, 1)
-        total = jnp.zeros((ROWS, 128), F32)
+        top, bottom = jnp.zeros((half, 128), F32), jnp.zeros((half, 128), F32)
         for j, vals in enumerate(pair(s.vals, cols, first_half())):
             h = 2 * tile + j
-            gaps = jnp.minimum(logs[:, j : j + 1] - s.logs_t[pl.ds(h, 1), :], 0.0)
-            decay = (jnp.exp(gaps) * s.dt_t[pl.ds(h, 1), :]).astype(BF16)
-            s.dec[h] = decay
-            mix = (s.scores[...] * decay.astype(F32)).astype(BF16)
-            total = total + dot(mix, vals, 1, 0)
-        s.inner[:, cols] = total
+            column, row, dt = logs[:, j : j + 1], s.logs_t[pl.ds(h, 1), :], s.dt_t[pl.ds(h, 1), :]
+            decay = (jnp.exp(jnp.minimum(column[:half] - row[:, :half], 0.0)) * dt[:, :half]).astype(BF16)
+            s.dec[h, :half, :half] = decay
+            mix = (s.scores[:half, :half] * decay.astype(F32)).astype(BF16)
+            top = top + dot(mix, vals[:half], 1, 0)
+            decay = (jnp.exp(jnp.minimum(column[half:] - row, 0.0)) * dt).astype(BF16)
+            s.dec[h, half:, :] = decay
+            mix = (s.scores[half:, :] * decay.astype(F32)).astype(BF16)
+            bottom = bottom + dot(mix, vals, 1, 0)
+        s.inner[:half, cols] = top
+        s.inner[half:, cols] = bottom
 
     tiles(low, high, body)
+
+
+def value_slopes(s):
+    def body(cols):
+        s.vsum[:, cols] = silu_slope(s.vsum[:, cols])
+
+    columns(body)
+    s.ssum[...] = silu_slope(s.ssum[...])
+
+
+def gate_slopes(s):
+    def body(cols):
+        gate = s.gate[:, cols]
+        sig = jax.nn.sigmoid(gate)
+        silu = gate * sig
+        s.gate[:, cols] = silu
+        s.gslope[:, cols] = (sig + silu * (1.0 - sig)).astype(BF16)
+
+    columns(body)
 
 
 def add_states(s):
@@ -696,8 +734,7 @@
         carried = dot(s.weight_top2[...], s.lanes[:, cols], 1, 0) + dot(s.weight_rest2[...], s.lanes[:, cols], 1, 0)
         inner = s.inner[:, cols] + dot(s.bc[:, STATE:], s.state[:, cols], 1, 0) * carried
         s.inner[:, cols] = inner
-        gate = s.gate[:, cols]
-        gated = (inner + s.skips[0:1, cols] * s.vals[:, cols].astype(F32)) * (gate * jax.nn.sigmoid(gate))
+        gated = (inner + s.skips[0:1, cols] * s.vals[:, cols].astype(F32)) * s.gate[:, cols]
         s.normal[:, cols] = gated
         s.squares[...] = s.squares[...] + gated * gated
 
@@ -743,12 +780,10 @@
     def body(cols):
         d_scaled = s.dout[:, cols] * s.gain_out[0:1, cols]
         d_gated = s.inverse[:, 0:1] * (d_scaled - s.normal[:, cols] * s.dots[:, 0:1])
-        gate = s.gate[:, cols]
-        sig = jax.nn.sigmoid(gate)
         vals = s.vals[:, cols].astype(F32)
         mixed = s.inner[:, cols] + s.skips[0:1, cols] * vals
-        d_mixed = d_gated * (gate * sig)
-        s.dgate[:, cols] = (d_gated * mixed * sig * (1.0 + gate * (1.0 - sig))).astype(BF16)
+        d_mixed = d_gated * s.gate[:, cols]
+        s.dgate[:, cols] = (d_gated * mixed * s.gslope[:, cols].astype(F32)).astype(BF16)
         s.small[6:7, cols] = jnp.sum(d_mixed * vals, axis=0, keepdims=True)
         s.dy[:, cols] = d_mixed.astype(BF16)
         s.dval[:, cols] = s.skips[0:1, cols] * d_mixed
@@ -766,17 +801,25 @@
 
 
 def mix_back(s, low, high):
+    half = ROWS // 2
+
     def body(tile, cols):
         total = jnp.zeros((ROWS, 128), F32)
-        d_scores = s.dscores[...]
+        top, bottom = s.dscores[:half, :half], s.dscores[half:, :]
+        blank = jnp.zeros((half, half), BF16)
         first = first_half()
         for j, (vals, grads) in enumerate(zip(pair(s.vals, cols, first), pair(s.dy, cols, first))):
             h = 2 * tile + j
-            d_mix = dot(grads, vals, 1, 1)
-            decay = s.dec[h].astype(F32)
-            d_scores = d_scores + d_mix * decay
-            total = total + dot((s.scores[...] * decay).astype(BF16), grads, 0, 0)
-        s.dscores[...] = d_scores
+            decay = s.dec[h, :half, :half].astype(F32)
+            top = top + dot(grads[:half], vals[:half], 1, 1) * decay
+            above = (s.scores[:half, :half] * decay).astype(BF16)
+            decay = s.dec[h, half:, :].astype(F32)
+            bottom = bottom + dot(grads[half:], vals, 1, 1) * decay
+            below = (s.scores[half:, :] * decay).astype(BF16)
+            mix = jnp.concatenate([jnp.concatenate([above, blank], axis=1), below], axis=0)
+            total = total + dot(mix, grads, 0, 0)
+        s.dscores[:half, :half] = top
+        s.dscores[half:, :] = bottom
         s.dval[:, cols] = s.dval[:, cols] + total
         s.dout[:, cols] = total * s.vals[:, cols].astype(F32)
 
@@ -811,7 +854,7 @@
         weights = dot(s.weight_top[...], lanes, 1, 0) + dot(s.weight_rest[...], lanes, 1, 0)
         weighted = s.vals[:, cols].astype(F32) * weights
         below = dot(s.bc[:, :STATE], s.coming[:, cols], 1, 0)
-        s.dsum[:ROWS, cols] = (s.dval[:, cols] + weights * below) * silu_slope(s.vsum[:, cols])
+        s.dsum[:ROWS, cols] = (s.dval[:, cols] + weights * below) * s.vsum[:, cols]
         s.through[...] = s.through[...] + to_heads(weighted * below, lanes)
         s.dbc[:, :STATE] = s.dbc[:, :STATE] + dot(weighted.astype(BF16), s.coming[:, cols], 1, 1)
 
@@ -831,7 +874,7 @@
     s.dstep[...] = d_step.astype(BF16)
     s.small[7:8, 0:128] = jnp.sum(d_step, axis=0, keepdims=True)
     s.small[7:8, 128:256] = jnp.sum(by_rate, axis=0, keepdims=True)
-    s.dsum[:ROWS, INNER:] = s.dbc[...] * silu_slope(s.ssum[...])
+    s.dsum[:ROWS, INNER:] = s.dbc[...] * s.ssum[...]
     s.edge[...] = s.dsum[0:8]
 
 
@@ -1012,7 +1055,7 @@
     scores=((ROWS, ROWS), F32), dscores=((ROWS, ROWS), F32), allowed=((ROWS, ROWS), F32),
     dec=((HEADS, ROWS, ROWS), BF16),
     inner=((ROWS, INNER), F32),
-    gate=((ROWS, INNER), F32), normal=((ROWS, INNER), F32),
+    gate=((ROWS, INNER), F32), gslope=((ROWS, INNER), BF16), normal=((ROWS, INNER), F32),
     inverse=((ROWS, 128), F32), nout=((ROWS, INNER), BF16), dout=((ROWS, INNER), F32),
     dgate=((ROWS, INNER), BF16), dy=((ROWS, INNER), BF16), dcar=((ROWS, INNER), BF16),
     direct=((ROWS, 128), F32), dlog=((ROWS, 128), F32),
@@ -1077,18 +1120,26 @@
     make_fresh(s)
     swap1 = Swap(me, s.fresh, s.fresh_in, sems.swap1)
     swap1.start()
+    mix_inside(s, 0, 4)
     gather_g.relay()
-    mix_inside(s, 0, 8)
+    mix_inside(s, 4, 10)
+    value_slopes(s)
+    gather_v.drain()
     swap1.wait()
     scan_states(s)
     swap2 = Swap(me, s.state_out, s.state_in, sems.swap2)
     swap2.start()
     gather_g.finish()
-    mix_inside(s, 8, 12)
+    mix_inside(s, 10, 12)
     gather_g.settle()
     for part in range(PARTS):
         s.gate[:, of_part(part)] = dot(s.normed[HALO:], weights_of(s.wg, part)[:, :WIDE], 1, 0)
         project_back(s, part)
+    gate_slopes(s)
+    swap1.drain()
+    for copy in [halo, *params]:
+        copy.wait_send()
+    gather_g.drain()
     swap2.wait()
     add_states(s)
     gated_norm(s)
@@ -1105,6 +1156,7 @@
     mix_back(s, 0, 2)
     reduce_g.relay()
     mix_back(s, 2, 6)
+    swap2.drain()
     swap3.wait()
     scan_back(s)
     swap4 = Swap(me, s.coming_out, s.coming_in, sems.swap4)
@@ -1114,14 +1166,18 @@
     mix_back(s, 8, 12)
     after_mix_back(s)
     normed_back_g(s)
+    swap3.drain()
     swap4.wait()
     leave(s)
     edge = transfer(s.edge, s.dsum.at[pl.ds(ROWS, 8)], sems.edges, 1, before)
     conv_grads(s)
+    swap4.drain()
     total = Total(me, s.small, s.small_sums, s.small_got, sems.total)
     total.along(0)
     reduce_g.second()
     edge.wait_recv()
+    total.add(0)
+    total.along(1)
     conv_back(s)
     parts_shared(s)
     shared = Shared(me, s.ps, s.heard_s, s.got_s, s.own_t, s.tails_in, sems.shared)
@@ -1130,10 +1186,10 @@
     reduce_v = reducer(me, ORDERS, s.pv, s.refs_v, sems.reduce_v)
     reduce_v.swap()
     shared.scatter()
+    total.add(1)
+    total.along(2)
     reduce_v.relay()
     reduce_v.third()
-    total.add(0)
-    total.along(1)
     normed_back_v(s)
     gain = Total(me, s.gain_row, s.gain_sums, s.gain_got, sems.total_gain)
     gain.along(0)
@@ -1141,14 +1197,12 @@
     shared.gather()
     gain.add(0)
     gain.along(1)
+    total.add(2)
+    total.along(3)
     reduce_v.second()
-    total.add(1)
-    total.along(2)
     gain.add(1)
     gain.along(2)
     reduce_v.first()
-    total.add(2)
-    total.along(3)
     gain.add(2)
     gain.along(3)
     shared.share()
@@ -1162,10 +1216,9 @@
     s.gains[...] = s.gain_sums[3]
     shared.finish()
 
-    for channel in (gather_v, gather_g, shared, reduce_g, reduce_v, total, gain, swap1, swap2, swap3, swap4):
+    for channel in (shared, reduce_g, reduce_v, total, gain):
         channel.drain()
-    for copy in [halo, edge, *params]:
-        copy.wait_send()
+    edge.wait_send()
 
 
 def kernel(*refs):

time: 109 us -> 106 us (0.972); the launches traced: 107 us -> 105 us
  Pallas kernels: 106 us -> 104 us
    pallas_call x1, Pallas kernels: 103 us -> 101 us  [shards(): pl.pallas_call(kernel, out_shape=shapes(RESULTS), in_specs=[smem if scala...]
where the time goes in v3:
time: 106 us; the launch traced here: 105 us
  Pallas kernels  104 us (98%)
    pallas_call x1, Pallas kernels, shards(): pl.pallas_call(kernel, out_shape=shapes(RESULTS), in_specs=[smem if scala...  101 us
    pallas_call x1, Pallas kernels, shards(): pl.pallas_call(closing_kernel, out_shape=shapes(OUTPUTS), in_specs=[vmem...  3.18 us

profile of v3, /device:TPU:1, one launch (start us, length us, event | category | flops | bytes accessed | tf_op | source)
XLA Modules:
  0.0 105.3 jit_solution(7539644750934250494)
XLA Ops:
  0.7 101.3 %shard_map.288 = (bf16[256,768]{1,0:T(8,128)(2,1)}, f32[256,768]{1,0:T(8,128)}, f32[48,256]{1,0:T(8,128)}, f32[48,384]{1,0:T(8,128)}, f32[8,1536]{1,0:T(8,128)},...) custom-call(bf16[256,768]{1,0:T(8,128)(2,1)} %refs_0_.1, bf16[256,768]{1,0:T(8,128)(2,1)} %refs_1_.1, ...), custom_call_target="tpu_custom_call" | custom-call | tf_op jit(solution)/shard_map/pallas_call | solution.py:1246
  101.9 3.2 %shard_map.289 = (bf16[256,768]{1,0:T(8,128)(2,1)}, f32[256,768]{1,0:T(8,128)}, f32[768]{0:T(1024)}, f32[48,192]{1,0:T(8,128)}, f32[48,192]{1,0:T(8,128)}, /*ind...) custom-call(bf16[256,768]{1,0:T(8,128)(2,1)} %get-tuple-element.39.r, ...), custom_call_target="tpu_custom_call" | custom-call | tf_op jit(solution)/shard_map/pallas_call | solution.py:1256
